TPU v7x, 128 devices: a whole 4x4x4 slice. The times are simulated.
128 devices in a mesh: row: 8 (over z, core), col: 16 (over y, x).
Axes of the slice: x: 4, y: 4, z: 4, core: 2. Of those that a mesh axis runs over, the one named last changes fastest.
Arguments:
- queries: bfloat16 [256, 1024], P(('row', 'col')), may hold values from -6 to 6
- lists: bfloat16 [256, 4096, 1024], P(('row', 'col')), may hold values from -6 to 6
- list_home: int32 [256], replicated, may hold values from 0 to 255, each once
- probes: int32 [256, 16], replicated, may hold values from 0 to 255, all different within a row; in each aligned block of 256 rows (0 to 255, 256 to 511, ...) at most 64 rows name the same one
- initials: bfloat16 [262144, 1024], P(('row', 'col')), may hold values from -6 to 6
- item_home: int32 [262144], replicated, may hold values from 0 to 262143, as said below
- cands: int32 [256, 100], replicated, may hold values from 0 to 262143, as said below
Outputs:
- mass: float32 [256, 16], P(('row', 'col'))
- rerank: float32 [256, 100], P(('row', 'col'))
Inputs may be any that keep to these rules, and one draw needn't show every extreme that they name: `probes`: each row names 16 different lists; no list is named by more than 64 rows, a bound that some block reaches. `list_home`: each number once. `item_home`: each number once. In each aligned block of 2 rows, the stored rows item_home[cands] fall into no aligned block of 2048 stored rows more than 2 times, and into some such block exactly 2 times.
All inputs are finite; a program needn't handle non-finite values.
Results may differ from a plain program's by a relative error of at most 0.00045.
Values may be sent and summed in bfloat16 or wider, within the bound.
No kernel may reach another device: no remote copies, remote signals or barrier semaphores. Data moves between devices by JAX's collectives and lax.ppermute only.
A program may use at most 64 MiB of HBM per device.

v0:
```python
import math

import jax
import jax.numpy as jnp
from jax import lax
from jax.sharding import PartitionSpec as P


def list_stat(query_rows, list_matrix, factor):
    total_rows = query_rows.shape[0]
    width = query_rows.shape[1]
    block_rows = min(512, total_rows)
    shaped = query_rows.reshape(total_rows // block_rows, block_rows, width)

    def block_stat(segment):
        scores = (
            lax.dot_general(
                segment, list_matrix, (((1,), (1,)), ((), ())), preferred_element_type=jnp.float32
            )
            * factor
        )
        return jnp.mean(jnp.square(jnp.maximum(scores, 0.0)), axis=1)

    return lax.map(block_stat, shaped).reshape(total_rows)


def local(queries, lists, list_home, probes, initials, item_home, cands):
    every_query = lax.all_gather(queries, ("row", "col"), axis=0, tiled=True)
    device = lax.axis_index(("row", "col"))
    held_lists = lists.shape[0]
    query_count = every_query.shape[0]
    factor = 1.0 / math.sqrt(every_query.shape[1])
    stored = jnp.take(list_home, probes, axis=0)
    totals = jnp.zeros(probes.shape, jnp.float32)
    for local_list in range(held_lists):
        list_index = device * held_lists + local_list
        hits = stored == list_index
        stats = list_stat(every_query, lists[local_list], factor)
        totals = totals + stats[:, None] * hits.astype(jnp.float32)
    mass = lax.psum_scatter(totals, ("row", "col"), scatter_dimension=0, tiled=True)
    held_items = initials.shape[0]
    homes = jnp.take(item_home, cands, axis=0)
    owner = homes // held_items
    offset = homes % held_items
    per_device = queries.shape[0]
    per_query = cands.shape[1]
    slot_count = per_device * per_query
    blocks = lax.axis_size(("row", "col"))
    spread = min(blocks, slot_count // 2)
    capacity = (slot_count + spread - 1) // spread
    owned_flat = (owner == device).reshape(-1)
    owned_total = jnp.sum(owned_flat.astype(jnp.int32))
    slot_limit = blocks * capacity
    positions = jnp.nonzero(owned_flat, size=slot_limit, fill_value=0)[0].astype(jnp.int32)
    live = jnp.arange(slot_limit, dtype=jnp.int32) < owned_total
    local_rows = jnp.take(offset.reshape(-1), positions, axis=0)
    item_rows = jnp.take(initials, local_rows, axis=0)
    query_rows = jnp.take(every_query, positions // per_query, axis=0)
    scored = jnp.einsum("nd,nd->n", item_rows, query_rows, preferred_element_type=jnp.float32)
    exact_terms = (
        jnp.zeros((query_count * per_query,), jnp.float32)
        .at[positions]
        .add(jnp.where(live, scored, jnp.float32(0.0)))
    )
    rerank = lax.psum_scatter(
        exact_terms.reshape(query_count, per_query), ("row", "col"), scatter_dimension=0, tiled=True
    )
    return (mass, rerank)


def solution(mesh):
    return jax.shard_map(
        local,
        mesh=mesh,
        in_specs=(
            P(("row", "col"), None),
            P(("row", "col"), None, None),
            P(),
            P(),
            P(("row", "col"), None),
            P(),
            P(),
        ),
        out_specs=(P(("row", "col"), None), P(("row", "col"), None)),
        check_vma=False,
    )
```

profile of v0, /device:TPU:1, one launch (start us, length us, event | category | flops | bytes accessed | tf_op | source)
XLA Modules:
  0.0 549.1 jit_solution(17883803600195225596)
XLA Ops:
  7.2 0.0 all-reduce.6.cloned.1.call-start
  7.2 1.1 copy.37
  8.3 0.1 reshape.313
  8.5 141.2 %gather_fusion.1 = s32[25600]{0:T(1024)S(1)} fusion(s32[262144]{0:T(1024)S(1)} %copy-done, s32[25600]{0:T(1024)S(1)} %broadcast_clamp_fusion), kind=kCustom, calls=%fused_computation.1 | custom fusion | bytes 307200 | tf_op jit(solution)/shard_map/jit(_take)/gather | solution.py:42
  149.7 0.2 reshape.312
  149.9 0.8 convert_reduce_fusion
  150.7 0.1 select_n.223
  150.8 0.1 select_n.232
  151.0 59.0 %all-gather = bf16[128,2,1024]{2,1,0:T(2,128)(2,1)S(1)} all-gather(bf16[1,2,1024]{2,1,0:T(2,128)(2,1)S(1)} %bitcast.49), channel_id=1, replica_groups=mesh['row'=8,'col'=16] {'row','col'}, dimensions={0}, use_global_device_ids=true | all-gather | bytes 528384 | tf_op jit(solution)/shard_map/all_gather | solution.py:28
  210.0 0.2 reshape.364
  210.2 0.1 fusion.38
  210.3 0.1 copy.40
  210.4 0.2 reduce-window.21
  210.6 0.3 reduce-window.24
  210.9 0.1 slice.32
  211.0 0.1 slice_reduce_fusion.1
  211.1 0.1 add_bitcast_fusion
  211.2 0.1 pad_slice_fusion
  211.3 0.1 copy.41
  211.4 0.1 compare_select_fusion
  211.5 176.9 %scatter_custom_fusion = s32[256]{0:T(256)S(1)} fusion(s32[25600]{0:T(1024)S(1)} %bitcast.46, s32[25600]{0:T(1024)S(1)} %broadcast.496, s32[]{:T(128)} %constant.170.clone.1), kind=kCustom, calls=%fused_computation.83 | custom fusion | flops 25600 | bytes 1028 | tf_op jit(solution)/shard_map/scatter-add | solution.py:54
  388.4 0.3 reduce-window.31
  388.7 0.1 slice.36
  388.9 0.1 slice_reduce_fusion
  389.0 0.7 compare_and_fusion
  389.7 0.7 compare_select_fusion.3
  390.5 1.7 gather_fusion.2
  392.2 0.7 compare_and_fusion.1
  392.9 1.2 gather_fusion.4
  394.1 4.3 gather_fusion.3
  398.4 0.4 fusion.30
  398.7 0.7 compare_select_fusion.11
  399.4 2.4 scatter_custom_fusion.1
  401.8 0.9 reshape.302
  402.7 0.0 all-reduce.6.cloned.1.call-update
  402.8 5.9 %fusion.27 = f32[256]{0:T(256)S(1)} fusion(bf16[256,1024]{1,0:T(8,128)(2,1)S(1)} %reshape.364, bf16[2,4096,1024]{2,1,0:T(8,128)(2,1)} %param.8), kind=kOutput, calls=%fused_computation.20 | convolution fusion | flops 2151677696 | bytes 8913920 | tf_op jit(solution)/shard_map/while/body/eval_jaxpr/dot_general | solution.py:17
  408.7 5.9 %fusion.24 = f32[256]{0:T(256)S(1)} fusion(bf16[256,1024]{1,0:T(8,128)(2,1)S(1)} %reshape.364, bf16[2,4096,1024]{2,1,0:T(8,128)(2,1)} %param.8), kind=kOutput, calls=%fused_computation.19 | convolution fusion | flops 2151677696 | bytes 8913920 | tf_op jit(solution)/shard_map/while/body/eval_jaxpr/dot_general | solution.py:17
  414.7 0.1 copy.34
  414.8 0.1 reshape.305
  414.9 0.4 copy-done.1
  415.3 25.7 %gather_fusion = s32[4096]{0:T(1024)S(1)} fusion(s32[256]{0:T(256)S(1)} %copy-done.1, s32[4096]{0:T(1024)S(1)} %broadcast_clamp_fusion.1), kind=kCustom, calls=%fused_computation | custom fusion | bytes 49152 | tf_op jit(solution)/shard_map/jit(_take)/gather | solution.py:33
  441.1 0.1 reshape.304
  441.1 0.1 copy.35
  441.2 0.1 copy.36
  441.3 65.6 %all-reduce.2 = f32[256,16]{1,0:T(8,128)S(1)} all-reduce(f32[256,16]{1,0:T(8,128)S(1)} %copy.36), channel_id=2, replica_groups=mesh['row'=8,'col'=16] {'row','col'}, use_global_device_ids=true, to_apply=%region_2.3.clone | all-reduce | flops 4096 | bytes 32768
  507.0 0.6 constant_dynamic-slice_fusion.1
  507.5 33.5 %all-reduce.6.cloned.1.call-done = f32[256,100]{1,0:T(8,128)} async-done(((f32[256,100]{1,0:T(8,128)}), f32[256,100]{1,0:T(8,128)}) %all-reduce.6.cloned.1.call-update) | async-done | bytes 102416
  541.0 1.2 constant_dynamic-slice_fusion
  (25 shorter events, 0.3 us)
Async XLA Ops:
  7.2 1.3 copy-start
  7.2 533.9 %all-reduce.6.cloned.1.call-start = ((), (), s32[]{:S(2)}) async-start(), calls=%async_computation | async-start | bytes 262144
  8.5 142.4 %copy-start.3 = (bf16[2,1024]{1,0:T(2,128)(2,1)S(1)}, bf16[2,1024]{1,0:T(2,128)(2,1)}, u32[]{:S(2)}) copy-start(bf16[2,1024]{1,0:T(2,128)(2,1)} %param.7) | copy-start | bytes 12292
  408.7 6.0 %copy-start.2 = (s32[256,16]{0,1:T(8,128)S(1)}, s32[256,16]{0,1:T(8,128)}, u32[]{:S(2)}) copy-start(s32[256,16]{0,1:T(8,128)} %param.10) | copy-start | bytes 49156
  414.6 0.7 copy-start.1
Sparse Core Ops, SparseCore 0:
  402.9 138.1 all-reduce.5
where the time goes:
time: 550 us; the launch traced here: 549 us
  other arithmetic  184 us (33%)
  local copies, waits for them, and re-layouts  180 us (33%)
  blocking collectives  125 us (23%)
  waiting for transfers between devices  33.5 us (6%)
  between operations  14.4 us (3%)
  matrix products  11.8 us (2%)
    scatter-add x1, other arithmetic, local(): jnp.nonzero(owned_flat, size=slot_limit, fill_value=0)[0].astype(jnp.int32)  177 us
    gather x2, local copies, waits for them, and re-layouts, local(): homes = jnp.take(item_home, cands, axis=0)  141 us
    unnamed x1, blocking collectives  65.6 us
    all_gather x1, blocking collectives, local(): every_query = lax.all_gather(queries, ('row', 'col'), axis=0, tiled=True)  59 us
    unnamed x2, waiting for transfers between devices  33.5 us
    gather x3, local copies, waits for them, and re-layouts, local(): stored = jnp.take(list_home, probes, axis=0)  25.9 us
    dot_general x2, matrix products, block_stat(): lax.dot_general(segment, list_matrix, (((1,), (1,)), ((), ())), preferred...  11.8 us
  transfers between devices with their start and end apart: 1, of which 1 were waited for; matrix products, arithmetic and copies ran while one was open for 7% of the time, Pallas kernels for 0%

commit v1 on v0

v1 whole, which is shorter than its diff:
```python
import math

import jax
import jax.numpy as jnp
from jax import lax
from jax.experimental import pallas as pl
from jax.experimental.pallas import tpu as pltpu
from jax.sharding import PartitionSpec as P

AXES = ("row", "col")
LANES = 128
CHUNK = 512


def pack_kernel(held_items, queries_ref, homes_ref, send_ref):
    rows, width = send_ref.shape[0], queries_ref.shape[1]
    queries = queries_ref[...].astype(jnp.float32)
    odd = lax.broadcasted_iota(jnp.int32, (rows, width), 0) % 2 == 1
    send_ref[:, :width] = jnp.where(odd, queries[1:2, :], queries[0:1, :]).astype(send_ref.dtype)
    homes = homes_ref[...]
    row = lax.broadcasted_iota(jnp.int32, (rows, LANES), 0)
    lane = lax.broadcasted_iota(jnp.int32, (rows, LANES), 1)
    home = jnp.where(row % 2 == 1, homes[1:2, :], homes[0:1, :])
    owned = home // held_items == row // 2
    key = (lane * held_items + home % held_items).astype(jnp.float32)
    big = float(LANES * held_items)
    first = jnp.min(jnp.where(owned, key, big), axis=1, keepdims=True)
    last = jnp.max(jnp.where(owned, key, -1.0), axis=1, keepdims=True)
    one = jnp.where(first < big, first.astype(jnp.int32) % held_items, -256)
    two = jnp.where(last > first, last.astype(jnp.int32) % held_items, -256)
    digits = jnp.where(
        lane == 0,
        one >> 8,
        jnp.where(lane == 1, one & 255, jnp.where(lane == 2, two >> 8, jnp.where(lane == 3, two & 255, 0))),
    )
    send_ref[:, width:] = digits.astype(jnp.float32).astype(send_ref.dtype)


def score_kernel(
    scale, got_ref, lists_ref, items_ref, out_ref, lists_v, items_v, list_sems, item_sems
):
    count, width = got_ref.shape[0], lists_ref.shape[2]
    held, list_rows = lists_ref.shape[0], lists_ref.shape[1]
    per_list = list_rows // CHUNK
    item_chunks = items_ref.shape[0] // CHUNK

    def list_copy(i, j):
        rows = pl.ds(pl.multiple_of(j * CHUNK, CHUNK), CHUNK)
        return pltpu.make_async_copy(lists_ref.at[i, rows], lists_v.at[i, rows], list_sems.at[i, j])

    def item_copy(j):
        rows = pl.ds(pl.multiple_of(j * CHUNK, CHUNK), CHUNK)
        return pltpu.make_async_copy(items_ref.at[rows], items_v.at[rows], item_sems.at[j])

    for i in range(held):
        for j in range(per_list):
            list_copy(i, j).start()
    for j in range(item_chunks):
        item_copy(j).start()

    queries = got_ref[:, :width]
    digits = jnp.transpose(got_ref[:, width:].astype(jnp.float32))
    one = (digits[0:1, :] * 256.0 + digits[1:2, :]).astype(jnp.int32)
    two = (digits[2:3, :] * 256.0 + digits[3:4, :]).astype(jnp.int32)

    def scores(block):
        return lax.dot_general(
            block, queries, (((1,), (1,)), ((), ())), preferred_element_type=jnp.float32
        )

    def fold(values):
        return jnp.sum(values.reshape(CHUNK // 8, 8, count), axis=0)

    zero = jnp.zeros((8, count), jnp.float32)
    results = []
    for i in range(held):

        def list_step(j, total, i=i):
            list_copy(i, j).wait()
            rows = pl.ds(pl.multiple_of(j * CHUNK, CHUNK), CHUNK)
            positive = jnp.maximum(scores(lists_v[i, rows, :]), 0.0)
            return total + fold(positive * positive)

        total = lax.fori_loop(0, per_list, list_step, zero)
        results.append(jnp.sum(total, axis=0, keepdims=True) * scale)

    def item_step(j, totals):
        item_copy(j).wait()
        rows = pl.ds(pl.multiple_of(j * CHUNK, CHUNK), CHUNK)
        found = scores(items_v[rows, :])
        index = lax.broadcasted_iota(jnp.int32, (CHUNK, count), 0) + j * CHUNK
        return (
            totals[0] + fold(jnp.where(index == one, found, 0.0)),
            totals[1] + fold(jnp.where(index == two, found, 0.0)),
        )

    for total in lax.fori_loop(0, item_chunks, item_step, (zero, zero)):
        results.append(jnp.sum(total, axis=0, keepdims=True))
    results.append(jnp.zeros((LANES - len(results), count), jnp.float32))
    out_ref[...] = jnp.transpose(jnp.concatenate(results, axis=0))


def place_kernel(held_items, held_lists, back_ref, homes_ref, stored_ref, mass_ref, rerank_ref):
    rows = back_ref.shape[0]
    per_query, probed = rerank_ref.shape[1], mass_ref.shape[1]
    back = back_ref[...]
    owner = homes_ref[...] // held_items
    stored = stored_ref[...]
    row = lax.broadcasted_iota(jnp.int32, (rows, LANES), 0)
    first = lax.broadcasted_iota(jnp.int32, (LANES, LANES), 0)
    second = lax.broadcasted_iota(jnp.int32, (LANES, LANES), 1)
    for a in range(2):
        own = owner[a : a + 1, :].astype(jnp.float32)
        down = jnp.sum(jnp.where(first == second, own, 0.0), axis=1, keepdims=True)
        earlier = jnp.where((down == own) & (first < second), 1.0, 0.0)
        rank = jnp.sum(earlier, axis=0, keepdims=True)
        value = jnp.where(rank > 0.5, back[:, held_lists + 1 : held_lists + 2], back[:, held_lists : held_lists + 1])
        mine = row == owner[a : a + 1, :] * 2 + a
        picked = jnp.sum(jnp.where(mine, value, 0.0), axis=0, keepdims=True)
        rerank_ref[a : a + 1, :] = picked[:, :per_query]
        place = stored[a : a + 1, :]
        value = jnp.where(place % held_lists == 1, back[:, 1:2], back[:, 0:1])
        mine = row == (place // held_lists) * 2 + a
        picked = jnp.sum(jnp.where(mine, value, 0.0), axis=0, keepdims=True)
        mass_ref[a : a + 1, :] = picked[:, :probed]


def local(queries, lists, list_home, probes, initials, item_home, cands):
    device = lax.axis_index(AXES)
    devices = lax.axis_size(AXES)
    mine, width = queries.shape
    held_lists, list_rows = lists.shape[0], lists.shape[1]
    held_items = initials.shape[0]
    per_query, probed = cands.shape[1], probes.shape[1]
    scale = 1.0 / (width * list_rows)

    own_cands = lax.dynamic_slice(cands, (device * mine, 0), (mine, per_query))
    own_probes = lax.dynamic_slice(probes, (device * mine, 0), (mine, probed))
    homes = item_home.at[own_cands].get(mode="promise_in_bounds")
    homes = jnp.pad(homes, ((0, 0), (0, LANES - per_query)), constant_values=-1)
    stored = list_home.at[own_probes].get(mode="promise_in_bounds")
    stored = jnp.pad(stored, ((0, 0), (0, LANES - probed)), constant_values=-1)

    send = pl.pallas_call(
        lambda *refs: pack_kernel(held_items, *refs),
        out_shape=jax.ShapeDtypeStruct((devices * mine, width + LANES), queries.dtype),
        name="pack",
    )(queries, homes)
    got = lax.all_to_all(send, AXES, 0, 0, tiled=True)
    results = pl.pallas_call(
        lambda *refs: score_kernel(scale, *refs),
        out_shape=jax.ShapeDtypeStruct((devices * mine, LANES), jnp.float32),
        in_specs=[
            pl.BlockSpec(memory_space=pltpu.VMEM),
            pl.BlockSpec(memory_space=pl.ANY),
            pl.BlockSpec(memory_space=pl.ANY),
        ],
        out_specs=pl.BlockSpec(memory_space=pltpu.VMEM),
        scratch_shapes=[
            pltpu.VMEM(lists.shape, lists.dtype),
            pltpu.VMEM(initials.shape, initials.dtype),
            pltpu.SemaphoreType.DMA((held_lists, list_rows // CHUNK)),
            pltpu.SemaphoreType.DMA((held_items // CHUNK,)),
        ],
        compiler_params=pltpu.CompilerParams(vmem_limit_bytes=40 * 1024 * 1024),
        cost_estimate=pl.CostEstimate(
            flops=2 * devices * mine * width * (held_lists * list_rows + held_items),
            bytes_accessed=2 * width * (held_lists * list_rows + held_items),
            transcendentals=0,
        ),
        name="score",
    )(got, lists, initials)
    back = lax.all_to_all(results, AXES, 0, 0, tiled=True)
    return pl.pallas_call(
        lambda *refs: place_kernel(held_items, held_lists, *refs),
        out_shape=(
            jax.ShapeDtypeStruct((mine, probed), jnp.float32),
            jax.ShapeDtypeStruct((mine, per_query), jnp.float32),
        ),
        name="place",
    )(back, homes, stored)


def solution(mesh):
    return jax.shard_map(
        local,
        mesh=mesh,
        in_specs=(P(AXES, None), P(AXES, None, None), P(), P(), P(AXES, None), P(), P()),
        out_specs=(P(AXES, None), P(AXES, None)),
        check_vma=False,
    )
```

time: 550 us -> 65.4 us (0.12)
  other arithmetic: 184 us -> 1.07 us
  local copies, waits for them, and re-layouts: 180 us -> 9.05 us
  blocking collectives: 125 us -> 25.9 us
  waiting for transfers between devices: 33.5 us -> 8.57 us
  Pallas kernels: 0 us -> 15.6 us
  between operations: 14.4 us -> 0.73 us
  matrix products: 11.8 us -> 0 us
    scatter-add x2 -> x0, other arithmetic: 179 us -> none  [the longest x1 177 us: local(): jnp.nonzero(owned_flat, size=slot_limit, fill_value=0)[0].astype(jnp.int32)]
    gather x8 -> x4, local copies, waits for them, and re-layouts: 174 us -> 2.6 us  [the longest x2 1.8 us: local(): homes = item_home.at[own_cands].get(mode='promise_in_bounds')]
    unnamed x1 -> x0, blocking collectives: 65.6 us -> none
    all_gather x1 -> x0, blocking collectives: 59 us -> none  [local(): every_query = lax.all_gather(queries, ('row', 'col'), axis=0, tiled=True)]
    unnamed x2 -> x0, waiting for transfers between devices: 33.5 us -> none
    all_to_all x0 -> x1, blocking collectives: none -> 25.9 us  [local(): got = lax.all_to_all(send, AXES, 0, 0, tiled=True)]
    pallas_call x0 -> x3, Pallas kernels: none -> 15.6 us  [the longest x1 11.9 us: local(): pl.pallas_call(lambda *refs: score_kernel(scale, *refs), out_shape=jax.Sh...]
    dot_general x2 -> x0, matrix products: 11.8 us -> none  [block_stat(): lax.dot_general(segment, list_matrix, (((1,), (1,)), ((), ())), preferred...]
  transfers between devices with their start and end apart: 1 -> 1, of which waited for: 1 -> 1; matrix products, arithmetic and copies ran while one was open for 7% -> 2% of each run, Pallas kernels for 0% -> 0%
where the time goes in v1:
time: 65.4 us; the launch traced here: 65.1 us
  blocking collectives  25.9 us (40%)
  Pallas kernels  15.6 us (24%)
  local copies, waits for them, and re-layouts  9.05 us (14%)
  waiting for transfers between devices  8.57 us (13%)
  starting transfers between devices  4.2 us (6%)
  other arithmetic  1.07 us (2%)
  between operations  0.73 us (1%)
    all_to_all x1, blocking collectives, local(): got = lax.all_to_all(send, AXES, 0, 0, tiled=True)  25.9 us
    pallas_call x1, Pallas kernels, local(): pl.pallas_call(lambda *refs: score_kernel(scale, *refs), out_shape=jax.Sh...  11.9 us
    all_to_all x1, waiting for transfers between devices, local(): back = lax.all_to_all(results, AXES, 0, 0, tiled=True)  8.57 us
    all_to_all x1, starting transfers between devices, local(): back = lax.all_to_all(results, AXES, 0, 0, tiled=True)  4.2 us
    unnamed x10, local copies, waits for them, and re-layouts  2.91 us
    all_to_all x2, local copies, waits for them, and re-layouts, local(): got = lax.all_to_all(send, AXES, 0, 0, tiled=True)  2.12 us
    pallas_call x1, Pallas kernels, local(): pl.pallas_call(lambda *refs: pack_kernel(held_items, *refs), out_shape=ja...  1.89 us
    pallas_call x1, Pallas kernels, local(): pl.pallas_call(lambda *refs: place_kernel(held_items, held_lists, *refs),...  1.8 us
  transfers between devices with their start and end apart: 1, of which 1 were waited for; matrix products, arithmetic and copies ran while one was open for 2% of the time, Pallas kernels for 0%

profile of v1, /device:TPU:1, one launch (start us, length us, event | category | flops | bytes accessed | tf_op | source)
XLA Modules:
  0.0 65.1 jit_solution(6825906305334175181)
XLA Ops:
  0.6 0.0 copy-start
  0.6 0.0 copy-start.4
  0.7 0.0 copy-start.2
  0.7 1.0 %compare_select_fusion = s32[2,100]{0,1:T(8,128)S(1)} fusion(s32[256,100]{0,1:T(8,128)} %param.13, s32[]{:T(128)S(6)} %select_n.10), kind=kLoop, calls=%fused_computation.2 | loop fusion | flops 600 | bytes 1604 | tf_op jit(solution)/shard_map/select_n | solution.py:139
  1.7 0.1 copy.10
  1.7 0.1 reshape.10
  1.8 0.1 copy-done
  1.9 1.7 %gather_fusion = s32[200]{0:T(256)S(1)} fusion(s32[262144]{0:T(1024)S(1)} %copy-done, s32[1024]{0:T(1024)S(1)} %pad_clamp_fusion.1), kind=kCustom, calls=%fused_computation | custom fusion | bytes 2400 | tf_op jit(solution)/shard_map/gather | solution.py:139
  3.6 0.1 reshape.9
  3.7 0.5 pad.8.refs_1_
  4.2 1.9 %pack.1 = bf16[256,1152]{1,0:T(8,128)(2,1)} custom-call(bf16[2,1024]{1,0:T(2,128)(2,1)} %refs_0_.1, s32[2,128]{1,0:T(2,128)} %pad.8.refs_1_), custom_call_target="tpu_custom_call" | custom-call | tf_op jit(solution)/shard_map/pack/pallas_call | solution.py:144
  6.1 1.9 %all_to_all.14 = bf16[128,2,1152]{2,1,0:T(2,128)(2,1)S(1)} reshape(bf16[256,1152]{1,0:T(8,128)(2,1)} %pack.1) | data formatting | bytes 1179648 | tf_op jit(solution)/shard_map/all_to_all | solution.py:149
  8.0 25.9 %all_to_all.22 = bf16[128,2,1152]{2,1,0:T(2,128)(2,1)S(1)} all-to-all(bf16[128,2,1152]{2,1,0:T(2,128)(2,1)S(1)} %all_to_all.14), channel_id=1, replica_groups=mesh['row'=8,'col'=16] {'row','col'}, dimensions={0} | all-to-all | bytes 1179648 | tf_op jit(solution)/shard_map/all_to_all | solution.py:149
  33.9 0.2 all_to_all.16.refs_0_
  34.2 0.0 copy-start.1
  34.2 2.2 %copy-done.1 = bf16[2048,1024]{1,0:T(8,128)(2,1)S(1)} copy-done((bf16[2048,1024]{1,0:T(8,128)(2,1)S(1)}, bf16[2048,1024]{1,0:T(8,128)(2,1)}, u32[]{:S(2)}) %copy-start.1) | copy-done | bytes 4194328
  36.3 11.9 %score.1 = f32[256,128]{1,0:T(8,128)} custom-call(bf16[256,1152]{1,0:T(8,128)(2,1)S(1)} %all_to_all.16.refs_0_, bf16[2,4096,1024]{2,1,0:T(8,128)(2,1)} %refs_1_.1, bf16[2048,1024]{1,0:T(8,128)(2,1)S(1)} %copy-done.1), custom_call_target="tpu_custom_call" | custom-call | flops 5368709120 | bytes 20971520 | tf_op jit(solution)/shard_map/score/pallas_call | solution.py:150
  48.2 4.2 %all-to-all-start.1 = ((f32[128,2,128]{2,1,0:T(2,128)}), f32[128,2,128]{2,1,0:T(2,128)S(1)}, u32[]{:S(2)}, u32[]{:S(2)}) async-start(f32[128,2,128]{2,1,0:T(2,128)} %bitcast), calls=%async_computation.1 | async-start | bytes 262144 | tf_op jit(solution)/shard_map/all_to_all | solution.py:173
  52.4 0.0 copy-done.4
  52.4 0.1 compare_select_fusion.1
  52.5 0.1 copy.11
  52.6 0.1 reshape.18
  52.7 0.0 copy-done.2
  52.7 0.7 %gather_fusion.1 = s32[32]{0:T(128)S(1)} fusion(s32[256]{0:T(256)S(1)} %copy-done.2, s32[1024]{0:T(1024)S(1)} %pad_clamp_fusion), kind=kCustom, calls=%fused_computation.1 | custom fusion | bytes 384 | tf_op jit(solution)/shard_map/gather | solution.py:141
  53.4 0.1 reshape.17
  53.5 0.6 pad.9.refs_2_
  54.1 8.6 %all-to-all-done.1 = f32[128,2,128]{2,1,0:T(2,128)S(1)} async-done(((f32[128,2,128]{2,1,0:T(2,128)}), f32[128,2,128]{2,1,0:T(2,128)S(1)}, u32[]{:S(2)}, u32[]{:S(2)}) %all-to-all-start.1) | async-done | bytes 131104 | tf_op jit(solution)/shard_map/all_to_all | solution.py:173
  62.6 0.0 copy-start.3
  62.6 0.6 copy-done.3
  63.3 1.8 %place.1 = (f32[2,16]{1,0:T(2,128)}, f32[2,100]{1,0:T(2,128)}) custom-call(f32[256,128]{1,0:T(8,128)} %bitcast.2, s32[2,128]{1,0:T(2,128)} %pad.8.refs_1_, s32[2,128]{1,0:T(2,128)} %pad.9.refs_2_), custom_call_target="tpu_custom_call" | custom-call | tf_op jit(solution)/shard_map/place/pallas_call | solution.py:174
  (2 shorter events, 0.0 us)
Async XLA Ops:
  0.6 1.3 %copy-start = (s32[262144]{0:T(1024)S(1)}, s32[262144]{0:T(1024)}, u32[]{:S(2)}) copy-start(s32[262144]{0:T(1024)} %param.12) | copy-start | bytes 3145732
  0.6 51.8 %copy-start.4 = (s32[256,16]{0,1:T(8,128)S(1)}, s32[256,16]{0,1:T(8,128)}, u32[]{:S(2)}) copy-start(s32[256,16]{0,1:T(8,128)} %param.10) | copy-start | bytes 49156
  0.7 52.1 %copy-start.2 = (s32[256]{0:T(256)S(1)}, s32[256]{0:T(256)}, u32[]{:S(2)}) copy-start(s32[256]{0:T(256)} %param.9) | copy-start | bytes 3076
  34.2 2.2 %copy-start.1 = (bf16[2048,1024]{1,0:T(8,128)(2,1)S(1)}, bf16[2048,1024]{1,0:T(8,128)(2,1)}, u32[]{:S(2)}) copy-start(bf16[2048,1024]{1,0:T(8,128)(2,1)} %refs_2_.1) | copy-start | bytes 12582916
  48.2 14.4 %all-to-all-start.1 = ((f32[128,2,128]{2,1,0:T(2,128)}), f32[128,2,128]{2,1,0:T(2,128)S(1)}, u32[]{:S(2)}, u32[]{:S(2)}) async-start(f32[128,2,128]{2,1,0:T(2,128)} %bitcast), calls=%async_computation.1 | async-start | bytes 262144 | tf_op jit(solution)/shard_map/all_to_all | solution.py:173
  62.6 0.6 copy-start.3

commit v2 on v1

v2 whole, which is shorter than its diff:
```python
import math

import jax
import jax.numpy as jnp
from jax import lax
from jax.experimental import pallas as pl
from jax.experimental.pallas import tpu as pltpu
from jax.sharding import PartitionSpec as P

AXES = ("row", "col")
LANES = 128
WHOLE = pl.BlockSpec(memory_space=pltpu.VMEM)
CHUNK = 512


def column_block(axes, mine):
    column = lax.axis_index(axes) * mine
    return pl.ds(pl.multiple_of(column // LANES * LANES, LANES), LANES), column % LANES


def column_of(block, place):
    lane = lax.broadcasted_iota(jnp.int32, block.shape, 1)
    return jnp.sum(jnp.where(lane == place, block, 0).astype(jnp.float32), axis=1, keepdims=True).astype(jnp.int32)


def homes_of(table_v, cands_v, cands_s, rows_v, place):
    for k in range(cands_v.shape[0]):
        rows_v[k : k + 1, :] = table_v[pl.ds(cands_s[k, place] // LANES, 1), :]
    return column_of(rows_v[...], column_of(cands_v[...], place) % LANES)


def pack_kernel(held_items, axes, queries_ref, cands_ref, table_ref, send_ref, queries_v, table_v, cands_v, cands_s, rows_v, sems):
    devices, mine, width = send_ref.shape[0], queries_ref.shape[0], queries_ref.shape[1]
    per_query = cands_ref.shape[0]
    block, place = column_block(axes, mine)
    copies = [
        pltpu.make_async_copy(cands_ref.at[:, block], cands_s, sems.at[0]),
        pltpu.make_async_copy(cands_ref.at[:, block], cands_v, sems.at[1]),
        pltpu.make_async_copy(table_ref, table_v, sems.at[2]),
        pltpu.make_async_copy(queries_ref, queries_v, sems.at[3]),
    ]
    for copy in copies:
        copy.start()
    copies[3].wait()
    send_ref[:, :, :width] = jnp.broadcast_to(queries_v[...][None], (devices, mine, width))
    for copy in copies[:3]:
        copy.wait()
    lane = lax.broadcasted_iota(jnp.int32, (per_query, LANES), 1)
    order = lax.broadcasted_iota(jnp.int32, (per_query, LANES), 0)
    big = float(per_query * held_items)
    digits = []
    for a in range(mine):
        home = homes_of(table_v, cands_v, cands_s, rows_v, place + a)
        key = (order * held_items + home % held_items).astype(jnp.float32)
        owned = home // held_items == lane
        first = jnp.min(jnp.where(owned, key, big), axis=0, keepdims=True)
        last = jnp.max(jnp.where(owned, key, -1.0), axis=0, keepdims=True)
        one = jnp.where(first < big, first.astype(jnp.int32) % held_items, -256)
        two = jnp.where(last > first, last.astype(jnp.int32) % held_items, -256)
        digits += [one >> 8, one & 255, two >> 8, two & 255]
    digits = [digit.astype(jnp.float32) for digit in digits]
    digits.append(jnp.zeros((LANES - len(digits), LANES), jnp.float32))
    digits = jnp.transpose(jnp.concatenate(digits, axis=0)).astype(send_ref.dtype)
    send_ref[:, :, width:] = jnp.broadcast_to(digits[:, None, :], (devices, mine, LANES))


def lookup_kernel(axes, mine, cands_ref, table_ref, probes_ref, list_home_ref, info_ref, table_v, cands_v, probes_v, list_home_v, cands_s, rows_v, sems):
    block, place = column_block(axes, mine)
    copies = [
        pltpu.make_async_copy(cands_ref.at[:, block], cands_s, sems.at[0]),
        pltpu.make_async_copy(cands_ref.at[:, block], cands_v, sems.at[1]),
        pltpu.make_async_copy(table_ref, table_v, sems.at[2]),
        pltpu.make_async_copy(probes_ref.at[:, block], probes_v, sems.at[3]),
        pltpu.make_async_copy(list_home_ref, list_home_v, sems.at[4]),
    ]
    for copy in copies:
        copy.start()
    for copy in copies:
        copy.wait()
    columns = [homes_of(table_v, cands_v, cands_s, rows_v, place + a) for a in range(mine)]
    for a in range(mine):
        ids = column_of(probes_v[...], place + a)
        stored = jnp.zeros_like(ids)
        for row in range(list_home_v.shape[0]):
            spread = jnp.broadcast_to(list_home_v[row : row + 1, :], (ids.shape[0], LANES))
            stored = stored + jnp.where(ids // LANES == row, column_of(spread, ids % LANES), 0)
        columns.append(stored)
    lane = lax.broadcasted_iota(jnp.int32, (LANES, LANES), 1)
    both = jnp.full((LANES, LANES), -1.0, jnp.float32)
    for j, column in enumerate(columns):
        column = column.astype(jnp.float32)
        short = jnp.full((LANES - column.shape[0], 1), -1.0, jnp.float32)
        both = jnp.where(lane == j, jnp.concatenate([column, short], axis=0), both)
    info_ref[...] = jnp.transpose(both)[: info_ref.shape[0], :].astype(jnp.int32)


def score_kernel(scale, got_ref, lists_ref, items_ref, out_ref):
    width, held, list_rows = lists_ref.shape[2], lists_ref.shape[0], lists_ref.shape[1]
    count = got_ref.shape[0] * got_ref.shape[1]
    got = got_ref[...].reshape(count, got_ref.shape[2])
    queries = got[:, :width]
    digits = jnp.transpose(got[:, width:].astype(jnp.float32))
    odd = lax.broadcasted_iota(jnp.int32, (1, count), 1) % 2 == 1
    digits = jnp.where(odd, digits[4:8, :], digits[0:4, :])
    one = (digits[0:1, :] * 256.0 + digits[1:2, :]).astype(jnp.int32)
    two = (digits[2:3, :] * 256.0 + digits[3:4, :]).astype(jnp.int32)

    def scores(block):
        return lax.dot_general(
            block, queries, (((1,), (1,)), ((), ())), preferred_element_type=jnp.float32
        )

    def fold(values):
        return jnp.sum(values.reshape(CHUNK // 8, 8, count), axis=0)

    results = []
    for i in range(held):
        total = jnp.zeros((8, count), jnp.float32)
        for start in range(0, list_rows, CHUNK):
            positive = jnp.maximum(scores(lists_ref[i, start : start + CHUNK, :]), 0.0)
            total = total + fold(positive * positive)
        results.append(jnp.sum(total, axis=0, keepdims=True) * scale)
    first = second = jnp.zeros((8, count), jnp.float32)
    for start in range(0, items_ref.shape[0], CHUNK):
        found = scores(items_ref[start : start + CHUNK, :])
        index = lax.broadcasted_iota(jnp.int32, (CHUNK, count), 0) + start
        first = first + fold(jnp.where(index == one, found, 0.0))
        second = second + fold(jnp.where(index == two, found, 0.0))
    results.append(jnp.sum(first, axis=0, keepdims=True))
    results.append(jnp.sum(second, axis=0, keepdims=True))
    results.append(jnp.zeros((LANES - len(results), count), jnp.float32))
    out_ref[...] = jnp.transpose(jnp.concatenate(results, axis=0))


def in_vmem(array):
    return pltpu.with_memory_space_constraint(array, pltpu.VMEM)


def in_hbm(array):
    return pltpu.with_memory_space_constraint(array, pltpu.HBM)


def place_kernel(held_items, held_lists, back_ref, info_ref, mass_ref, rerank_ref):
    rows = back_ref.shape[0]
    per_query, probed = rerank_ref.shape[1], mass_ref.shape[1]
    back = back_ref[...]
    owner = info_ref[0:2, :] // held_items
    stored = info_ref[2:4, :]
    row = lax.broadcasted_iota(jnp.int32, (rows, LANES), 0)
    first = lax.broadcasted_iota(jnp.int32, (LANES, LANES), 0)
    second = lax.broadcasted_iota(jnp.int32, (LANES, LANES), 1)
    for a in range(2):
        own = owner[a : a + 1, :].astype(jnp.float32)
        down = jnp.sum(jnp.where(first == second, own, 0.0), axis=1, keepdims=True)
        earlier = jnp.where((down == own) & (first < second), 1.0, 0.0)
        rank = jnp.sum(earlier, axis=0, keepdims=True)
        value = jnp.where(rank > 0.5, back[:, held_lists + 1 : held_lists + 2], back[:, held_lists : held_lists + 1])
        mine = row == owner[a : a + 1, :] * 2 + a
        picked = jnp.sum(jnp.where(mine, value, 0.0), axis=0, keepdims=True)
        rerank_ref[a : a + 1, :] = picked[:, :per_query]
        place = stored[a : a + 1, :]
        value = jnp.where(place % held_lists == 1, back[:, 1:2], back[:, 0:1])
        mine = row == (place // held_lists) * 2 + a
        picked = jnp.sum(jnp.where(mine, value, 0.0), axis=0, keepdims=True)
        mass_ref[a : a + 1, :] = picked[:, :probed]


def local(queries, lists, list_home, probes, initials, item_home, cands):
    devices = lax.axis_size(AXES)
    mine, width = queries.shape
    held_lists, list_rows = lists.shape[0], lists.shape[1]
    held_items = initials.shape[0]
    per_query, probed = cands.shape[1], probes.shape[1]
    scale = 1.0 / (width * list_rows)

    table = item_home.reshape(-1, LANES)
    send = pl.pallas_call(
        lambda *refs: pack_kernel(held_items, AXES, *refs),
        out_shape=pltpu.VMEM((devices, mine, width + LANES), queries.dtype),
        in_specs=[pl.BlockSpec(memory_space=pltpu.HBM)] * 3,
        out_specs=WHOLE,
        scratch_shapes=[
            pltpu.VMEM(queries.shape, queries.dtype),
            pltpu.VMEM((item_home.shape[0] // LANES, LANES), jnp.int32),
            pltpu.VMEM((per_query, LANES), jnp.int32),
            pltpu.SMEM((per_query, LANES), jnp.int32),
            pltpu.VMEM((per_query, LANES), jnp.int32),
            pltpu.SemaphoreType.DMA((4,)),
        ],
        compiler_params=pltpu.CompilerParams(vmem_limit_bytes=4 * 1024 * 1024),
        cost_estimate=pl.CostEstimate(flops=1<<36, bytes_accessed=1<<28, transcendentals=0),
        name="pack",
    )(in_hbm(queries), in_hbm(cands.T), in_hbm(table))
    got = lax.all_to_all(send, AXES, 0, 0, tiled=True)
    results = pl.pallas_call(
        lambda *refs: score_kernel(scale, *refs),
        out_shape=pltpu.VMEM((devices * mine, LANES), jnp.float32),
        in_specs=[WHOLE] * 3,
        out_specs=WHOLE,
        compiler_params=pltpu.CompilerParams(vmem_limit_bytes=16 * 1024 * 1024),
        cost_estimate=pl.CostEstimate(
            flops=2 * devices * mine * width * (held_lists * list_rows + held_items),
            bytes_accessed=2 * width * (held_lists * list_rows + held_items),
            transcendentals=0,
        ),
        name="score",
    )(in_vmem(got), in_vmem(lists), in_vmem(initials))
    results, table, late_cands, late_probes, homes = lax.optimization_barrier(
        (results, table, cands.T, probes.T, list_home.reshape(-1, LANES))
    )
    info = pl.pallas_call(
        lambda *refs: lookup_kernel(AXES, mine, *refs),
        out_shape=pltpu.VMEM((8, LANES), jnp.int32),
        in_specs=[pl.BlockSpec(memory_space=pltpu.HBM)] * 4,
        out_specs=WHOLE,
        scratch_shapes=[
            pltpu.VMEM(table.shape, jnp.int32),
            pltpu.VMEM((per_query, LANES), jnp.int32),
            pltpu.VMEM((probed, LANES), jnp.int32),
            pltpu.VMEM(homes.shape, jnp.int32),
            pltpu.SMEM((per_query, LANES), jnp.int32),
            pltpu.VMEM((per_query, LANES), jnp.int32),
            pltpu.SemaphoreType.DMA((5,)),
        ],
        compiler_params=pltpu.CompilerParams(vmem_limit_bytes=4 * 1024 * 1024),
        cost_estimate=pl.CostEstimate(flops=0, bytes_accessed=2 * 1024 * 1024, transcendentals=0),
        name="lookup",
    )(in_hbm(late_cands), in_hbm(table), in_hbm(late_probes), in_hbm(homes))
    back = lax.all_to_all(results, AXES, 0, 0, tiled=True)
    return pl.pallas_call(
        lambda *refs: place_kernel(held_items, held_lists, *refs),
        out_shape=(
            jax.ShapeDtypeStruct((mine, probed), jnp.float32),
            jax.ShapeDtypeStruct((mine, per_query), jnp.float32),
        ),
        name="place",
    )(in_vmem(back), in_vmem(info))


def solution(mesh):
    return jax.shard_map(
        local,
        mesh=mesh,
        in_specs=(P(AXES, None), P(AXES, None, None), P(), P(), P(AXES, None), P(), P()),
        out_specs=(P(AXES, None), P(AXES, None)),
        check_vma=False,
    )
```

time: 65.4 us -> 51.6 us (0.79)
  local copies, waits for them, and re-layouts: 9.05 us -> 0.01 us
  Pallas kernels: 15.6 us -> 13.3 us
  waiting for transfers between devices: 8.57 us -> 7.33 us
  other arithmetic: 1.07 us -> 0 us
    unnamed x10 -> x4, local copies, waits for them, and re-layouts: 2.91 us -> 0.01 us
    gather x4 -> x0, local copies, waits for them, and re-layouts: 2.6 us -> none  [the longest x2 1.8 us: local(): homes = item_home.at[own_cands].get(mode='promise_in_bounds')]
    all_to_all x2 -> x0, local copies, waits for them, and re-layouts: 2.12 us -> none  [local(): got = lax.all_to_all(send, AXES, 0, 0, tiled=True)]
    pallas_call x2 -> x3, Pallas kernels: 13.8 us -> 12.4 us  [the longest x1 6.59 us: local(): pl.pallas_call(lambda *refs: score_kernel(scale, *refs), out_shape=pltpu....]
    all_to_all x1, waiting for transfers between devices: 8.57 us -> 7.33 us  [local(): back = lax.all_to_all(results, AXES, 0, 0, tiled=True)]
    pad x2 -> x0, local copies, waits for them, and re-layouts: 1.1 us -> none  [the longest x1 0.56 us: local(): stored = jnp.pad(stored, ((0, 0), (0, LANES - probed)), constant_values=-1)]
    select_n x2 -> x0, other arithmetic: 1.05 us -> none  [the longest x1 0.97 us: local(): homes = item_home.at[own_cands].get(mode='promise_in_bounds')]
    pallas_call x1, Pallas kernels: 1.8 us -> 0.89 us  [local(): pl.pallas_call(lambda *refs: place_kernel(held_items, held_lists, *refs),...]
  transfers between devices with their start and end apart: 1 -> 1, of which waited for: 1 -> 1; matrix products, arithmetic and copies ran while one was open for 2% -> 0% of each run, Pallas kernels for 0% -> 5%
where the time goes in v2:
time: 51.6 us; the launch traced here: 51.4 us
  blocking collectives  25.9 us (50%)
  Pallas kernels  13.3 us (26%)
  waiting for transfers between devices  7.33 us (14%)
  starting transfers between devices  4.16 us (8%)
  between operations  0.67 us (1%)
    all_to_all x1, blocking collectives, local(): got = lax.all_to_all(send, AXES, 0, 0, tiled=True)  25.9 us
    all_to_all x1, waiting for transfers between devices, local(): back = lax.all_to_all(results, AXES, 0, 0, tiled=True)  7.33 us
    pallas_call x1, Pallas kernels, local(): pl.pallas_call(lambda *refs: score_kernel(scale, *refs), out_shape=pltpu....  6.59 us
    all_to_all x1, starting transfers between devices, local(): back = lax.all_to_all(results, AXES, 0, 0, tiled=True)  4.16 us
    pallas_call x1, Pallas kernels, local(): pl.pallas_call(lambda *refs: pack_kernel(held_items, AXES, *refs), out_sh...  3.02 us
    pallas_call x1, Pallas kernels, local(): pl.pallas_call(lambda *refs: lookup_kernel(AXES, mine, *refs), out_shape=...  2.82 us
  transfers between devices with their start and end apart: 1, of which 1 were waited for; matrix products, arithmetic and copies ran while one was open for 0% of the time, Pallas kernels for 5%

profile of v2, /device:TPU:1, one launch (start us, length us, event | category | flops | bytes accessed | tf_op | source)
XLA Modules:
  0.0 51.4 jit_solution(4457603036129219640)
XLA Ops:
  0.6 0.0 copy-start
  0.6 0.0 copy-start.1
  0.6 3.0 %pack.1 = bf16[128,2,1152]{2,1,0:T(2,128)(2,1)S(1)} custom-call(bf16[2,1024]{1,0:T(2,128)(2,1)} %refs_0_.1, s32[100,256]{1,0:T(8,128)} %bitcast.9, s32[2048,128]{1,0:T(8,128)} %bitcast.7), custom_call_target="tpu_custom_call" | custom-call | flops 68719476736 | bytes 268435456 | tf_op jit(solution)/shard_map/pack/pallas_call | solution.py:177
  3.7 25.9 %all_to_all.16.refs_0_ = bf16[128,2,1152]{2,1,0:T(2,128)(2,1)S(1)} all-to-all(bf16[128,2,1152]{2,1,0:T(2,128)(2,1)S(1)} %pack.1), channel_id=1, replica_groups=mesh['row'=8,'col'=16] {'row','col'}, dimensions={0} | all-to-all | bytes 1179648 | tf_op jit(solution)/shard_map/all_to_all | solution.py:194
  29.6 0.0 copy-done
  29.6 0.0 copy-done.1
  29.6 6.6 %score.1 = f32[256,128]{1,0:T(8,128)} custom-call(bf16[128,2,1152]{2,1,0:T(2,128)(2,1)S(1)} %all_to_all.16.refs_0_, bf16[2,4096,1024]{2,1,0:T(8,128)(2,1)S(1)} %copy-done, bf16[2048,1024]{1,0:T(8,128)(2,1)S(1)} %copy-done.1), custom_call_target="tpu_custom_call" | custom-call | flops 5368709120 | bytes 20971520 | tf_op jit(solution)/shard_map/score/pallas_call | solution.py:195
  36.2 4.2 %all-to-all-start.1 = ((f32[128,2,128]{2,1,0:T(2,128)}), f32[128,2,128]{2,1,0:T(2,128)S(1)}, u32[]{:S(2)}, u32[]{:S(2)}) async-start(f32[128,2,128]{2,1,0:T(2,128)} %bitcast.4), calls=%async_computation.1 | async-start | bytes 262144 | tf_op jit(solution)/shard_map/all_to_all | solution.py:229
  40.3 2.8 %lookup.1.refs_1_ = s32[8,128]{1,0:T(8,128)S(1)} custom-call(s32[100,256]{1,0:T(8,128)} %bitcast.10, s32[2048,128]{1,0:T(8,128)} %bitcast.8, s32[16,256]{1,0:T(8,128)} %bitcast.11, s32[2,128]{1,0:T(2,128)} %bitcast.12), custom_call_target="tpu_custom_call" | custom-call | bytes 2097152 | tf_op jit(solution)/shard_map/lookup/pallas_call | solution.py:211
  43.2 7.3 %all-to-all-done.1 = f32[128,2,128]{2,1,0:T(2,128)S(1)} async-done(((f32[128,2,128]{2,1,0:T(2,128)}), f32[128,2,128]{2,1,0:T(2,128)S(1)}, u32[]{:S(2)}, u32[]{:S(2)}) %all-to-all-start.1) | async-done | bytes 131104 | tf_op jit(solution)/shard_map/all_to_all | solution.py:229
  50.5 0.9 %place.1 = (f32[2,16]{1,0:T(2,128)}, f32[2,100]{1,0:T(2,128)}) custom-call(f32[256,128]{1,0:T(8,128)S(1)} %bitcast.6, s32[8,128]{1,0:T(8,128)S(1)} %lookup.1.refs_1_), custom_call_target="tpu_custom_call" | custom-call | tf_op jit(solution)/shard_map/place/pallas_call | solution.py:230
Async XLA Ops:
  0.6 28.9 %copy-start = (bf16[2,4096,1024]{2,1,0:T(8,128)(2,1)S(1)}, bf16[2,4096,1024]{2,1,0:T(8,128)(2,1)}, u32[]{:S(2)}) copy-start(bf16[2,4096,1024]{2,1,0:T(8,128)(2,1)} %refs_1_.1) | copy-start | bytes 50331652
  0.6 28.9 %copy-start.1 = (bf16[2048,1024]{1,0:T(8,128)(2,1)S(1)}, bf16[2048,1024]{1,0:T(8,128)(2,1)}, u32[]{:S(2)}) copy-start(bf16[2048,1024]{1,0:T(8,128)(2,1)} %refs_2_.1) | copy-start | bytes 12582916
  36.2 14.3 %all-to-all-start.1 = ((f32[128,2,128]{2,1,0:T(2,128)}), f32[128,2,128]{2,1,0:T(2,128)S(1)}, u32[]{:S(2)}, u32[]{:S(2)}) async-start(f32[128,2,128]{2,1,0:T(2,128)} %bitcast.4), calls=%async_computation.1 | async-start | bytes 262144 | tf_op jit(solution)/shard_map/all_to_all | solution.py:229

commit v3 on v2

v3 whole, which is shorter than its diff:
```python
import math

import jax
import jax.numpy as jnp
from jax import lax
from jax.experimental import pallas as pl
from jax.experimental.pallas import tpu as pltpu
from jax.sharding import PartitionSpec as P

AXES = ("row", "col")
LANES = 128
WHOLE = pl.BlockSpec(memory_space=pltpu.VMEM)
CHUNK = 1024
EARLY = 3072


def column_block(axes, mine):
    column = lax.axis_index(axes) * mine
    start = pl.multiple_of((column >> 7) * LANES, LANES)
    return pl.ds(start, LANES), column & (LANES - 1)


def column_of(block, place):
    lane = lax.broadcasted_iota(jnp.int32, block.shape, 1)
    return jnp.sum(jnp.where(lane == place, block, 0).astype(jnp.float32), axis=1, keepdims=True).astype(jnp.int32)


def homes_of(table_v, cands_v, cands_s, rows_v, place):
    for k in range(cands_v.shape[0]):
        rows_v[k : k + 1, :] = table_v[pl.ds(cands_s[k, place] >> 7, 1), :]
    return column_of(rows_v[...], column_of(cands_v[...], place) & (LANES - 1))


def pack_kernel(held_items, axes, run, queries_ref, cands_ref, table_ref, send_ref, queries_v, table_v, cands_v, cands_s, rows_v, sems):
    devices, mine, width = send_ref.shape[0], queries_ref.shape[0], queries_ref.shape[1]
    per_query = cands_ref.shape[0]
    block, place = column_block(axes, mine)
    copies = [
        pltpu.make_async_copy(cands_ref.at[:, block], cands_s, sems.at[0]),
        pltpu.make_async_copy(cands_ref.at[:, block], cands_v, sems.at[1]),
        pltpu.make_async_copy(table_ref, table_v, sems.at[2]),
        pltpu.make_async_copy(queries_ref, queries_v, sems.at[3]),
    ]
    for copy in copies:
        copy.start()
    copies[3].wait()
    half = width // 2
    for start in range(0, devices, run):
        part = start // run % 2 * half
        send_ref[start : start + run, :, :half] = jnp.broadcast_to(queries_v[:, part : part + half][None], (run, mine, half))
    for copy in copies[:3]:
        copy.wait()
    lane = lax.broadcasted_iota(jnp.int32, (per_query, LANES), 1)
    order = lax.broadcasted_iota(jnp.int32, (per_query, LANES), 0)
    big = float(per_query * held_items)
    shift = held_items.bit_length() - 1
    digits = []
    for a in range(mine):
        home = homes_of(table_v, cands_v, cands_s, rows_v.at[a], place + a)
        key = (order * held_items + (home & (held_items - 1))).astype(jnp.float32)
        owned = home >> shift == lane
        first = jnp.min(jnp.where(owned, key, big), axis=0, keepdims=True)
        last = jnp.max(jnp.where(owned, key, -1.0), axis=0, keepdims=True)
        one = jnp.where(first < big, first.astype(jnp.int32) & (held_items - 1), -256)
        two = jnp.where(last > first, last.astype(jnp.int32) & (held_items - 1), -256)
        digits += [one >> 8, one & 255, two >> 8, two & 255]
    digits = [digit.astype(jnp.float32) for digit in digits]
    digits.append(jnp.zeros((LANES - len(digits), LANES), jnp.float32))
    digits = jnp.transpose(jnp.concatenate(digits, axis=0)).astype(send_ref.dtype)
    send_ref[:, :, half:] = jnp.broadcast_to(digits[:, None, :], (devices, mine, LANES))


def lookup_kernel(axes, mine, cands_ref, table_ref, probes_ref, list_home_ref, info_ref, table_v, cands_v, probes_v, list_home_v, cands_s, rows_v, sems):
    block, place = column_block(axes, mine)
    copies = [
        pltpu.make_async_copy(cands_ref.at[:, block], cands_s, sems.at[0]),
        pltpu.make_async_copy(cands_ref.at[:, block], cands_v, sems.at[1]),
        pltpu.make_async_copy(table_ref, table_v, sems.at[2]),
        pltpu.make_async_copy(probes_ref.at[:, block], probes_v, sems.at[3]),
        pltpu.make_async_copy(list_home_ref, list_home_v, sems.at[4]),
    ]
    for copy in copies:
        copy.start()
    for copy in copies:
        copy.wait()
    columns = [homes_of(table_v, cands_v, cands_s, rows_v.at[a], place + a) for a in range(mine)]
    for a in range(mine):
        ids = column_of(probes_v[...], place + a)
        stored = jnp.zeros_like(ids)
        for row in range(list_home_v.shape[0]):
            spread = jnp.broadcast_to(list_home_v[row : row + 1, :], (ids.shape[0], LANES))
            stored = stored + jnp.where(ids >> 7 == row, column_of(spread, ids & (LANES - 1)), 0)
        columns.append(stored)
    lane = lax.broadcasted_iota(jnp.int32, (LANES, LANES), 1)
    both = jnp.full((LANES, LANES), -1.0, jnp.float32)
    for j, column in enumerate(columns):
        column = column.astype(jnp.float32)
        short = jnp.full((LANES - column.shape[0], 1), -1.0, jnp.float32)
        both = jnp.where(lane == j, jnp.concatenate([column, short], axis=0), both)
    info_ref[...] = jnp.transpose(both)[: info_ref.shape[0], :].astype(jnp.int32)


def scores(block, queries):
    return lax.dot_general(block, queries, (((1,), (1,)), ((), ())), preferred_element_type=jnp.float32)


def early_kernel(got_ref, lists_ref, items_ref, part_ref):
    count, half = got_ref.shape[0] * got_ref.shape[1], lists_ref.shape[2] // 2
    mine = got_ref[...].reshape(count, got_ref.shape[2])[:, :half]
    own = pl.ds(pl.multiple_of((lax.axis_index("row") & 1) * half, half), half)
    held_items = items_ref.shape[0]
    for start in range(0, held_items, CHUNK):
        part_ref[start : start + CHUNK, :] = scores(items_ref[start : start + CHUNK, own], mine)
    for start in range(0, EARLY, CHUNK):
        to = slice(held_items + start, held_items + start + CHUNK)
        part_ref[to, :] = scores(lists_ref[0, start : start + CHUNK, own], mine)


def score_kernel(scale, got_ref, other_ref, part_ref, lists_ref, items_ref, out_ref, wide_ref):
    width, held, list_rows = lists_ref.shape[2], lists_ref.shape[0], lists_ref.shape[1]
    count = got_ref.shape[0] * got_ref.shape[1]
    got = got_ref[...].reshape(count, got_ref.shape[2])
    other = other_ref[...].reshape(got.shape)
    half = width // 2
    mine, theirs = got[:, :half], other[:, :half]
    core = lax.axis_index("row") & 1
    queries = jnp.concatenate([jnp.where(core == 0, mine, theirs), jnp.where(core == 0, theirs, mine)], axis=1)
    rest = pl.ds(pl.multiple_of((1 - core) * half, half), half)
    digits = jnp.transpose(got[:, half:].astype(jnp.float32))
    odd = lax.broadcasted_iota(jnp.int32, (1, count), 1) & 1 == 1
    digits = jnp.where(odd, digits[4:8, :], digits[0:4, :])
    one = (digits[0:1, :] * 256.0 + digits[1:2, :]).astype(jnp.int32)
    two = (digits[2:3, :] * 256.0 + digits[3:4, :]).astype(jnp.int32)

    def fold(values):
        return jnp.sum(values.reshape(CHUNK // 8, 8, count), axis=0)

    results = []
    for i in range(held):
        total = jnp.zeros((8, count), jnp.float32)
        for start in range(0, list_rows, CHUNK):
            rows = slice(start, start + CHUNK)
            if i == 0 and start < EARLY:
                done = slice(items_ref.shape[0] + start, items_ref.shape[0] + start + CHUNK)
                found = part_ref[done, :] + scores(lists_ref[i, rows, rest], theirs)
            else:
                found = scores(lists_ref[i, rows, :], queries)
            positive = jnp.maximum(found, 0.0)
            total = total + fold(positive * positive)
        results.append(jnp.sum(total, axis=0, keepdims=True) * scale)
    first = second = jnp.zeros((8, count), jnp.float32)
    for start in range(0, items_ref.shape[0], CHUNK):
        rows = slice(start, start + CHUNK)
        found = part_ref[rows, :] + scores(items_ref[rows, rest], theirs)
        index = lax.broadcasted_iota(jnp.int32, (CHUNK, count), 0) + start
        first = first + fold(jnp.where(index == one, found, 0.0))
        second = second + fold(jnp.where(index == two, found, 0.0))
    results.append(jnp.sum(first, axis=0, keepdims=True))
    results.append(jnp.sum(second, axis=0, keepdims=True))
    results = jnp.concatenate(results, axis=0)
    results = jnp.concatenate([results, pltpu.roll(results, count - 1, 1)], axis=0)
    results = jnp.concatenate([results, jnp.zeros((LANES - results.shape[0], count), jnp.float32)], axis=0)
    wide_ref[...] = jnp.transpose(results)
    out_ref[...] = wide_ref[pl.ds(0, out_ref.shape[0], stride=2), :]


def in_vmem(array):
    return pltpu.with_memory_space_constraint(array, pltpu.VMEM)


def in_hbm(array):
    return pltpu.with_memory_space_constraint(array, pltpu.HBM)


def place_kernel(held_items, held_lists, back_ref, info_ref, mass_ref, rerank_ref):
    rows = back_ref.shape[0]
    per_query, probed = rerank_ref.shape[1], mass_ref.shape[1]
    back = back_ref[...]
    owner = info_ref[0:2, :] >> (held_items.bit_length() - 1)
    stored = info_ref[2:4, :]
    row = lax.broadcasted_iota(jnp.int32, (rows, LANES), 0)
    first = lax.broadcasted_iota(jnp.int32, (LANES, LANES), 0)
    second = lax.broadcasted_iota(jnp.int32, (LANES, LANES), 1)
    for a in range(2):
        own = owner[a : a + 1, :].astype(jnp.float32)
        down = jnp.sum(jnp.where(first == second, own, 0.0), axis=1, keepdims=True)
        earlier = jnp.where((down == own) & (first < second), 1.0, 0.0)
        rank = jnp.sum(earlier, axis=0, keepdims=True)
        at = a * (held_lists + 2)
        value = jnp.where(rank > 0.5, back[:, at + held_lists + 1 : at + held_lists + 2], back[:, at + held_lists : at + held_lists + 1])
        picked = jnp.sum(jnp.where(row == owner[a : a + 1, :], value, 0.0), axis=0, keepdims=True)
        rerank_ref[a : a + 1, :] = picked[:, :per_query]
        place = stored[a : a + 1, :]
        value = jnp.where(place & 1 == 1, back[:, at + 1 : at + 2], back[:, at : at + 1])
        picked = jnp.sum(jnp.where(row == place >> 1, value, 0.0), axis=0, keepdims=True)
        mass_ref[a : a + 1, :] = picked[:, :probed]


def local(queries, lists, list_home, probes, initials, item_home, cands):
    devices = lax.axis_size(AXES)
    mine, width = queries.shape
    held_lists, list_rows = lists.shape[0], lists.shape[1]
    held_items = initials.shape[0]
    per_query, probed = cands.shape[1], probes.shape[1]
    scale = 1.0 / (width * list_rows)

    run = lax.axis_size("col")
    table = item_home.reshape(-1, LANES)
    send = pl.pallas_call(
        lambda *refs: pack_kernel(held_items, AXES, run, *refs),
        out_shape=pltpu.VMEM((devices, mine, width // 2 + LANES), queries.dtype),
        in_specs=[pl.BlockSpec(memory_space=pltpu.HBM)] * 3,
        out_specs=WHOLE,
        scratch_shapes=[
            pltpu.VMEM(queries.shape, queries.dtype),
            pltpu.VMEM((item_home.shape[0] // LANES, LANES), jnp.int32),
            pltpu.VMEM((per_query, LANES), jnp.int32),
            pltpu.SMEM((per_query, LANES), jnp.int32),
            pltpu.VMEM((mine, per_query, LANES), jnp.int32),
            pltpu.SemaphoreType.DMA((4,)),
        ],
        compiler_params=pltpu.CompilerParams(vmem_limit_bytes=4 * 1024 * 1024),
        cost_estimate=pl.CostEstimate(flops=1<<36, bytes_accessed=1<<28, transcendentals=0),
        name="pack",
    )(in_hbm(queries), in_hbm(cands.T), in_hbm(table))
    got = lax.all_to_all(send, AXES, 0, 0, tiled=True)
    pairs = [(i, i ^ 1) for i in range(lax.axis_size("row"))]
    other = lax.ppermute(got, "row", pairs)
    part = pl.pallas_call(
        early_kernel,
        out_shape=pltpu.VMEM((held_items + EARLY, devices * mine), jnp.float32),
        in_specs=[WHOLE] * 3,
        out_specs=WHOLE,
        compiler_params=pltpu.CompilerParams(vmem_limit_bytes=8 * 1024 * 1024),
        cost_estimate=pl.CostEstimate(
            flops=devices * mine * width * (held_items + EARLY),
            bytes_accessed=width * (held_items + EARLY), transcendentals=0,
        ),
        name="early",
    )(in_vmem(got), in_vmem(lists), in_vmem(initials))
    results = pl.pallas_call(
        lambda *refs: score_kernel(scale, *refs),
        out_shape=pltpu.VMEM((devices, LANES), jnp.float32),
        scratch_shapes=[pltpu.VMEM((devices * mine, LANES), jnp.float32)],
        in_specs=[WHOLE] * 5,
        out_specs=WHOLE,
        compiler_params=pltpu.CompilerParams(vmem_limit_bytes=16 * 1024 * 1024),
        cost_estimate=pl.CostEstimate(
            flops=2 * devices * mine * width * (held_lists * list_rows + held_items),
            bytes_accessed=2 * width * (held_lists * list_rows + held_items),
            transcendentals=0,
        ),
        name="score",
    )(in_vmem(got), in_vmem(other), in_vmem(part), in_vmem(lists), in_vmem(initials))
    results, table, late_cands, late_probes, homes = lax.optimization_barrier(
        (results, table, cands.T, probes.T, list_home.reshape(-1, LANES))
    )
    info = pl.pallas_call(
        lambda *refs: lookup_kernel(AXES, mine, *refs),
        out_shape=pltpu.VMEM((8, LANES), jnp.int32),
        in_specs=[pl.BlockSpec(memory_space=pltpu.HBM)] * 4,
        out_specs=WHOLE,
        scratch_shapes=[
            pltpu.VMEM(table.shape, jnp.int32),
            pltpu.VMEM((per_query, LANES), jnp.int32),
            pltpu.VMEM((probed, LANES), jnp.int32),
            pltpu.VMEM(homes.shape, jnp.int32),
            pltpu.SMEM((per_query, LANES), jnp.int32),
            pltpu.VMEM((mine, per_query, LANES), jnp.int32),
            pltpu.SemaphoreType.DMA((5,)),
        ],
        compiler_params=pltpu.CompilerParams(vmem_limit_bytes=4 * 1024 * 1024),
        cost_estimate=pl.CostEstimate(flops=0, bytes_accessed=2 * 1024 * 1024, transcendentals=0),
        name="lookup",
    )(in_hbm(late_cands), in_hbm(table), in_hbm(late_probes), in_hbm(homes))
    back = lax.all_to_all(results[:, None, :], AXES, 0, 0, tiled=True)[:, 0, :]
    return pl.pallas_call(
        lambda *refs: place_kernel(held_items, held_lists, *refs),
        out_shape=(
            jax.ShapeDtypeStruct((mine, probed), jnp.float32),
            jax.ShapeDtypeStruct((mine, per_query), jnp.float32),
        ),
        name="place",
    )(in_vmem(back), in_vmem(info))


def solution(mesh):
    return jax.shard_map(
        local,
        mesh=mesh,
        in_specs=(P(AXES, None), P(AXES, None, None), P(), P(), P(AXES, None), P(), P()),
        out_specs=(P(AXES, None), P(AXES, None)),
        check_vma=False,
    )
```

time: 51.6 us -> 48.1 us (0.932)
  blocking collectives: 25.9 us -> 23.2 us
  Pallas kernels: 13.3 us -> 12.1 us
    all_to_all x1, blocking collectives: 25.9 us -> 23.2 us  [local(): got = lax.all_to_all(send, AXES, 0, 0, tiled=True)]
    pallas_call x1, Pallas kernels: 6.59 us -> 5.3 us  [local(): pl.pallas_call(lambda *refs: score_kernel(scale, *refs), out_shape=pltpu....]
    pallas_call x1 -> x2, Pallas kernels: 3.02 us -> 3.81 us  [the longest x1 2.25 us: local(): pl.pallas_call(lambda *refs: pack_kernel(held_items, AXES, run, *refs), o...]
    pallas_call x1, Pallas kernels: 2.82 us -> 2.07 us  [local(): pl.pallas_call(lambda *refs: lookup_kernel(AXES, mine, *refs), out_shape=...]
    ppermute x0 -> x1, starting transfers between devices: none -> 0.7 us  [local(): other = lax.ppermute(got, 'row', pairs)]
    all_to_all x1, starting transfers between devices: 4.16 us -> 3.63 us  [local(): back = lax.all_to_all(results[:, None, :], AXES, 0, 0, tiled=True)[:, 0, :]]
  transfers between devices with their start and end apart: 1 -> 2, of which waited for: 1 -> 1; matrix products, arithmetic and copies ran while one was open for 0% -> 0% of each run, Pallas kernels for 5% -> 8%
where the time goes in v3:
time: 48.1 us; the launch traced here: 47.9 us
  blocking collectives  23.2 us (48%)
  Pallas kernels  12.1 us (25%)
  waiting for transfers between devices  7.52 us (16%)
  starting transfers between devices  4.33 us (9%)
  between operations  0.73 us (2%)
    all_to_all x1, blocking collectives, local(): got = lax.all_to_all(send, AXES, 0, 0, tiled=True)  23.2 us
    all_to_all x1, waiting for transfers between devices, local(): back = lax.all_to_all(results[:, None, :], AXES, 0, 0, tiled=True)[:, 0, :]  7.52 us
    pallas_call x1, Pallas kernels, local(): pl.pallas_call(lambda *refs: score_kernel(scale, *refs), out_shape=pltpu....  5.3 us
    all_to_all x1, starting transfers between devices, local(): back = lax.all_to_all(results[:, None, :], AXES, 0, 0, tiled=True)[:, 0, :]  3.63 us
    pallas_call x1, Pallas kernels, local(): pl.pallas_call(lambda *refs: pack_kernel(held_items, AXES, run, *refs), o...  2.25 us
    pallas_call x1, Pallas kernels, local(): pl.pallas_call(lambda *refs: lookup_kernel(AXES, mine, *refs), out_shape=...  2.07 us
    pallas_call x1, Pallas kernels, local(): pl.pallas_call(early_kernel, out_shape=pltpu.VMEM((held_items + EARLY, de...  1.56 us
  transfers between devices with their start and end apart: 2, of which 1 were waited for; matrix products, arithmetic and copies ran while one was open for 0% of the time, Pallas kernels for 8%

profile of v3, /device:TPU:1, one launch (start us, length us, event | category | flops | bytes accessed | tf_op | source)
XLA Modules:
  0.0 47.9 jit_solution(281972956924701734)
XLA Ops:
  0.6 0.0 slice-start
  0.6 0.0 slice-start.1
  0.7 0.0 slice-start.2
  0.7 0.0 slice-start.3
  0.7 0.0 copy-start
  0.7 2.2 %pack.1 = bf16[128,2,640]{2,1,0:T(2,128)(2,1)S(1)} custom-call(bf16[2,1024]{1,0:T(2,128)(2,1)} %refs_0_.1, s32[100,256]{1,0:T(8,128)} %bitcast.13, s32[2048,128]{1,0:T(8,128)} %bitcast.11), custom_call_target="tpu_custom_call" | custom-call | flops 68719476736 | bytes 268435456 | tf_op jit(solution)/shard_map/pack/pallas_call | solution.py:209
  2.9 23.2 %all_to_all.10.got_ref.refs_0_ = bf16[128,2,640]{2,1,0:T(2,128)(2,1)S(1)} all-to-all(bf16[128,2,640]{2,1,0:T(2,128)(2,1)S(1)} %pack.1), channel_id=1, replica_groups=mesh['row'=8,'col'=16] {'row','col'}, dimensions={0} | all-to-all | bytes 655360 | tf_op jit(solution)/shard_map/all_to_all | solution.py:226
  26.2 0.7 %collective-permute-start = (bf16[128,2,640]{2,1,0:T(2,128)(2,1)S(1)}, bf16[128,2,640]{2,1,0:T(2,128)(2,1)S(1)}, u32[]{:S(2)}, u32[]{:S(2)}) collective-permute-start(bf16[128,2,640]{2,1,0:T(2,128)(2,1)S(1)} %all_to_all.10.got_ref.refs_0_), channel_id=1, source_target_pairs={{0,16},{16,0},{32,48},{48,32},{64,80},{80,64},{96,112},{112,96},{1... | collective-permute-start | bytes 983048 | tf_op jit(solution)/shard_map/ppermute | solution.py:228
  26.9 0.0 slice-done
  26.9 0.0 slice-done.1
  26.9 0.0 slice-done.2
  26.9 0.0 slice-done.3
  26.9 0.0 copy-done
  26.9 1.6 %early.1.refs_2_ = f32[5120,256]{1,0:T(8,128)S(1)} custom-call(bf16[128,2,640]{2,1,0:T(2,128)(2,1)S(1)} %all_to_all.10.got_ref.refs_0_, bf16[2,4096,1024]{2,1,0:T(8,128)(2,1)S(1)} %bitcast.9, bf16[2048,1024]{1,0:T(8,128)(2,1)S(1)} %copy-done), custom_call_target="tpu_custom_call" | custom-call | flops 1342177280 | bytes 5242880 | tf_op jit(solution)/shard_map/early/pallas_call | solution.py:229
  28.5 0.0 collective-permute-done.refs_1_
  28.5 5.3 %score.1 = f32[128,128]{1,0:T(8,128)} custom-call(bf16[128,2,640]{2,1,0:T(2,128)(2,1)S(1)} %all_to_all.10.got_ref.refs_0_, bf16[128,2,640]{2,1,0:T(2,128)(2,1)S(1)} %collective-permute-done.refs_1_, f32[5120,256]{1,0:T(8,128)S(1)} %early.1.refs_2_, bf16[2,4096,1024]{2,1,0:T(8,128)(2,1)S(1)} %bitcast.9, bf16[2048,1024]{1,0:T(8,128)(2,1)S(1)} %copy-done), custom_call_target="tpu_custom_call" | custom-call | flops 5368709120 | bytes 20971520 | tf_op jit(solution)/shard_map/score/pallas_call | solution.py:241
  33.8 3.6 %all-to-all-start.1 = ((f32[128,1,128]{2,1,0:T(1,128)}), f32[128,1,128]{2,1,0:T(1,128)S(1)}, u32[]{:S(2)}, u32[]{:S(2)}) async-start(f32[128,1,128]{2,1,0:T(1,128)} %bitcast.5), calls=%async_computation.1 | async-start | bytes 131072 | tf_op jit(solution)/shard_map/all_to_all | solution.py:276
  37.4 2.1 %lookup.1.refs_1_ = s32[8,128]{1,0:T(8,128)S(1)} custom-call(s32[100,256]{1,0:T(8,128)} %bitcast.14, s32[2048,128]{1,0:T(8,128)} %bitcast.12, s32[16,256]{1,0:T(8,128)} %bitcast.15, s32[2,128]{1,0:T(2,128)} %bitcast.16), custom_call_target="tpu_custom_call" | custom-call | bytes 2097152 | tf_op jit(solution)/shard_map/lookup/pallas_call | solution.py:258
  39.5 7.5 %all-to-all-done.1 = f32[128,1,128]{2,1,0:T(1,128)S(1)} async-done(((f32[128,1,128]{2,1,0:T(1,128)}), f32[128,1,128]{2,1,0:T(1,128)S(1)}, u32[]{:S(2)}, u32[]{:S(2)}) %all-to-all-start.1) | async-done | bytes 65568 | tf_op jit(solution)/shard_map/all_to_all | solution.py:276
  47.0 0.9 %place.1 = (f32[2,16]{1,0:T(2,128)}, f32[2,100]{1,0:T(2,128)}) custom-call(f32[128,128]{1,0:T(8,128)S(1)} %bitcast.10, s32[8,128]{1,0:T(8,128)S(1)} %lookup.1.refs_1_), custom_call_target="tpu_custom_call" | custom-call | tf_op jit(solution)/shard_map/place/pallas_call | solution.py:277
  (1 shorter events, 0.0 us)
Async XLA Ops:
  0.6 26.2 %slice-start = ((s8[16777216]{0:T(1024)(128)(4,1)}), s8[4194304]{0:T(1024)(128)(4,1)S(1)}, s32[]{:S(2)}) async-start(s8[16777216]{0:T(1024)(128)(4,1)} %bitcast.8), calls=%async_computation.2 | async-start | bytes 8388608
  0.6 26.2 %slice-start.1 = ((s8[16777216]{0:T(1024)(128)(4,1)}), s8[4194304]{0:T(1024)(128)(4,1)S(1)}, s32[]{:S(2)}) async-start(s8[16777216]{0:T(1024)(128)(4,1)} %bitcast.8), calls=%async_computation.3 | async-start | bytes 8388608
  0.7 26.2 %slice-start.2 = ((s8[16777216]{0:T(1024)(128)(4,1)}), s8[4194304]{0:T(1024)(128)(4,1)S(1)}, s32[]{:S(2)}) async-start(s8[16777216]{0:T(1024)(128)(4,1)} %bitcast.8), calls=%async_computation.4 | async-start | bytes 8388608
  0.7 26.2 %slice-start.3 = ((s8[16777216]{0:T(1024)(128)(4,1)}), s8[4194304]{0:T(1024)(128)(4,1)S(1)}, s32[]{:S(2)}) async-start(s8[16777216]{0:T(1024)(128)(4,1)} %bitcast.8), calls=%async_computation.5 | async-start | bytes 8388608
  0.7 26.2 %copy-start = (bf16[2048,1024]{1,0:T(8,128)(2,1)S(1)}, bf16[2048,1024]{1,0:T(8,128)(2,1)}, u32[]{:S(2)}) copy-start(bf16[2048,1024]{1,0:T(8,128)(2,1)} %refs_4_.1) | copy-start | bytes 12582916
  26.2 2.3 %collective-permute-start = (bf16[128,2,640]{2,1,0:T(2,128)(2,1)S(1)}, bf16[128,2,640]{2,1,0:T(2,128)(2,1)S(1)}, u32[]{:S(2)}, u32[]{:S(2)}) collective-permute-start(bf16[128,2,640]{2,1,0:T(2,128)(2,1)S(1)} %all_to_all.10.got_ref.refs_0_), channel_id=1, source_target_pairs={{0,16},{16,0},{32,48},{48,32},{64,80},{80,64},{96,112},{112,96},{1... | collective-permute-start | bytes 983048 | tf_op jit(solution)/shard_map/ppermute | solution.py:228
  33.8 13.2 %all-to-all-start.1 = ((f32[128,1,128]{2,1,0:T(1,128)}), f32[128,1,128]{2,1,0:T(1,128)S(1)}, u32[]{:S(2)}, u32[]{:S(2)}) async-start(f32[128,1,128]{2,1,0:T(1,128)} %bitcast.5), calls=%async_computation.1 | async-start | bytes 131072 | tf_op jit(solution)/shard_map/all_to_all | solution.py:276

commit v4 on v3

--- a/solution.py
+++ b/solution.py
@@ -70,7 +70,7 @@
     send_ref[:, :, half:] = jnp.broadcast_to(digits[:, None, :], (devices, mine, LANES))
 
 
-def lookup_kernel(axes, mine, cands_ref, table_ref, probes_ref, list_home_ref, info_ref, table_v, cands_v, probes_v, list_home_v, cands_s, rows_v, sems):
+def lookup_kernel(held_items, axes, mine, cands_ref, table_ref, probes_ref, list_home_ref, info_ref, table_v, cands_v, probes_v, list_home_v, cands_s, rows_v, sems):
     block, place = column_block(axes, mine)
     copies = [
         pltpu.make_async_copy(cands_ref.at[:, block], cands_s, sems.at[0]),
@@ -97,7 +97,20 @@
         column = column.astype(jnp.float32)
         short = jnp.full((LANES - column.shape[0], 1), -1.0, jnp.float32)
         both = jnp.where(lane == j, jnp.concatenate([column, short], axis=0), both)
-    info_ref[...] = jnp.transpose(both)[: info_ref.shape[0], :].astype(jnp.int32)
+    rows = jnp.transpose(both)[: 2 * mine, :].astype(jnp.int32)
+    shift = held_items.bit_length() - 1
+    per_query = cands_v.shape[0]
+    before = lax.broadcasted_iota(jnp.int32, (per_query, LANES), 0) < lax.broadcasted_iota(
+        jnp.int32, (per_query, LANES), 1
+    )
+    info = []
+    for a in range(mine):
+        owner = rows[a : a + 1, :] >> shift
+        earlier = (columns[a] >> shift == owner) & before
+        info += [owner, jnp.sum(earlier.astype(jnp.float32), axis=0, keepdims=True).astype(jnp.int32)]
+        stored = rows[mine + a : mine + a + 1, :]
+        info += [stored >> 1, stored & 1]
+    info_ref[...] = jnp.concatenate(info, axis=0)
 
 
 def scores(block, queries):
@@ -172,28 +185,20 @@
     return pltpu.with_memory_space_constraint(array, pltpu.HBM)
 
 
-def place_kernel(held_items, held_lists, back_ref, info_ref, mass_ref, rerank_ref):
-    rows = back_ref.shape[0]
+def place_kernel(held_lists, back_ref, info_ref, mass_ref, rerank_ref):
     per_query, probed = rerank_ref.shape[1], mass_ref.shape[1]
     back = back_ref[...]
-    owner = info_ref[0:2, :] >> (held_items.bit_length() - 1)
-    stored = info_ref[2:4, :]
-    row = lax.broadcasted_iota(jnp.int32, (rows, LANES), 0)
-    first = lax.broadcasted_iota(jnp.int32, (LANES, LANES), 0)
-    second = lax.broadcasted_iota(jnp.int32, (LANES, LANES), 1)
+    row = lax.broadcasted_iota(jnp.int32, (back.shape[0], LANES), 0)
+
+    def picked(at, a, j):
+        owner, later = info_ref[4 * a + j : 4 * a + j + 1, :], info_ref[4 * a + j + 1 : 4 * a + j + 2, :]
+        value = jnp.where(later > 0, back[:, at + 1 : at + 2], back[:, at : at + 1])
+        return jnp.sum(jnp.where(row == owner, value, 0.0), axis=0, keepdims=True)
+
     for a in range(2):
-        own = owner[a : a + 1, :].astype(jnp.float32)
-        down = jnp.sum(jnp.where(first == second, own, 0.0), axis=1, keepdims=True)
-        earlier = jnp.where((down == own) & (first < second), 1.0, 0.0)
-        rank = jnp.sum(earlier, axis=0, keepdims=True)
         at = a * (held_lists + 2)
-        value = jnp.where(rank > 0.5, back[:, at + held_lists + 1 : at + held_lists + 2], back[:, at + held_lists : at + held_lists + 1])
-        picked = jnp.sum(jnp.where(row == owner[a : a + 1, :], value, 0.0), axis=0, keepdims=True)
-        rerank_ref[a : a + 1, :] = picked[:, :per_query]
-        place = stored[a : a + 1, :]
-        value = jnp.where(place & 1 == 1, back[:, at + 1 : at + 2], back[:, at : at + 1])
-        picked = jnp.sum(jnp.where(row == place >> 1, value, 0.0), axis=0, keepdims=True)
-        mass_ref[a : a + 1, :] = picked[:, :probed]
+        rerank_ref[a : a + 1, :] = picked(at + held_lists, a, 0)[:, :per_query]
+        mass_ref[a : a + 1, :] = picked(at, a, 2)[:, :probed]
 
 
 def local(queries, lists, list_home, probes, initials, item_home, cands):
@@ -256,7 +261,7 @@
         (results, table, cands.T, probes.T, list_home.reshape(-1, LANES))
     )
     info = pl.pallas_call(
-        lambda *refs: lookup_kernel(AXES, mine, *refs),
+        lambda *refs: lookup_kernel(held_items, AXES, mine, *refs),
         out_shape=pltpu.VMEM((8, LANES), jnp.int32),
         in_specs=[pl.BlockSpec(memory_space=pltpu.HBM)] * 4,
         out_specs=WHOLE,
@@ -275,7 +280,7 @@
     )(in_hbm(late_cands), in_hbm(table), in_hbm(late_probes), in_hbm(homes))
     back = lax.all_to_all(results[:, None, :], AXES, 0, 0, tiled=True)[:, 0, :]
     return pl.pallas_call(
-        lambda *refs: place_kernel(held_items, held_lists, *refs),
+        lambda *refs: place_kernel(held_lists, *refs),
         out_shape=(
             jax.ShapeDtypeStruct((mine, probed), jnp.float32),
             jax.ShapeDtypeStruct((mine, per_query), jnp.float32),

time: 48.1 us -> 48 us (level)
  no operation moved by 1% of the time
where the time goes in v4:
time: 48 us; the launch traced here: 47.8 us
  blocking collectives  23.2 us (48%)
  Pallas kernels  12 us (25%)
  waiting for transfers between devices  7.5 us (16%)
  starting transfers between devices  4.33 us (9%)
  between operations  0.73 us (2%)
    all_to_all x1, blocking collectives, local(): got = lax.all_to_all(send, AXES, 0, 0, tiled=True)  23.2 us
    all_to_all x1, waiting for transfers between devices, local(): back = lax.all_to_all(results[:, None, :], AXES, 0, 0, tiled=True)[:, 0, :]  7.5 us
    pallas_call x1, Pallas kernels, local(): pl.pallas_call(lambda *refs: score_kernel(scale, *refs), out_shape=pltpu....  5.3 us
    all_to_all x1, starting transfers between devices, local(): back = lax.all_to_all(results[:, None, :], AXES, 0, 0, tiled=True)[:, 0, :]  3.63 us
    pallas_call x1, Pallas kernels, local(): pl.pallas_call(lambda *refs: pack_kernel(held_items, AXES, run, *refs), o...  2.25 us
    pallas_call x1, Pallas kernels, local(): pl.pallas_call(lambda *refs: lookup_kernel(held_items, AXES, mine, *refs)...  2.09 us
    pallas_call x1, Pallas kernels, local(): pl.pallas_call(early_kernel, out_shape=pltpu.VMEM((held_items + EARLY, de...  1.56 us
  transfers between devices with their start and end apart: 2, of which 1 were waited for; matrix products, arithmetic and copies ran while one was open for 0% of the time, Pallas kernels for 8%

profile of v4, /device:TPU:1, one launch (start us, length us, event | category | flops | bytes accessed | tf_op | source)
XLA Modules:
  0.0 47.8 jit_solution(11257827994643388373)
XLA Ops:
  0.6 0.0 slice-start
  0.6 0.0 slice-start.1
  0.7 0.0 slice-start.2
  0.7 0.0 slice-start.3
  0.7 0.0 copy-start
  0.7 2.2 %pack.1 = bf16[128,2,640]{2,1,0:T(2,128)(2,1)S(1)} custom-call(bf16[2,1024]{1,0:T(2,128)(2,1)} %refs_0_.1, s32[100,256]{1,0:T(8,128)} %bitcast.13, s32[2048,128]{1,0:T(8,128)} %bitcast.11), custom_call_target="tpu_custom_call" | custom-call | flops 68719476736 | bytes 268435456 | tf_op jit(solution)/shard_map/pack/pallas_call | solution.py:214
  2.9 23.2 %all_to_all.10.got_ref.refs_0_ = bf16[128,2,640]{2,1,0:T(2,128)(2,1)S(1)} all-to-all(bf16[128,2,640]{2,1,0:T(2,128)(2,1)S(1)} %pack.1), channel_id=1, replica_groups=mesh['row'=8,'col'=16] {'row','col'}, dimensions={0} | all-to-all | bytes 655360 | tf_op jit(solution)/shard_map/all_to_all | solution.py:231
  26.2 0.7 %collective-permute-start = (bf16[128,2,640]{2,1,0:T(2,128)(2,1)S(1)}, bf16[128,2,640]{2,1,0:T(2,128)(2,1)S(1)}, u32[]{:S(2)}, u32[]{:S(2)}) collective-permute-start(bf16[128,2,640]{2,1,0:T(2,128)(2,1)S(1)} %all_to_all.10.got_ref.refs_0_), channel_id=1, source_target_pairs={{0,16},{16,0},{32,48},{48,32},{64,80},{80,64},{96,112},{112,96},{1... | collective-permute-start | bytes 983048 | tf_op jit(solution)/shard_map/ppermute | solution.py:233
  26.9 0.0 slice-done
  26.9 0.0 slice-done.1
  26.9 0.0 slice-done.2
  26.9 0.0 slice-done.3
  26.9 0.0 copy-done
  26.9 1.6 %early.1.refs_2_ = f32[5120,256]{1,0:T(8,128)S(1)} custom-call(bf16[128,2,640]{2,1,0:T(2,128)(2,1)S(1)} %all_to_all.10.got_ref.refs_0_, bf16[2,4096,1024]{2,1,0:T(8,128)(2,1)S(1)} %bitcast.9, bf16[2048,1024]{1,0:T(8,128)(2,1)S(1)} %copy-done), custom_call_target="tpu_custom_call" | custom-call | flops 1342177280 | bytes 5242880 | tf_op jit(solution)/shard_map/early/pallas_call | solution.py:234
  28.5 0.0 collective-permute-done.refs_1_
  28.5 5.3 %score.1 = f32[128,128]{1,0:T(8,128)} custom-call(bf16[128,2,640]{2,1,0:T(2,128)(2,1)S(1)} %all_to_all.10.got_ref.refs_0_, bf16[128,2,640]{2,1,0:T(2,128)(2,1)S(1)} %collective-permute-done.refs_1_, f32[5120,256]{1,0:T(8,128)S(1)} %early.1.refs_2_, bf16[2,4096,1024]{2,1,0:T(8,128)(2,1)S(1)} %bitcast.9, bf16[2048,1024]{1,0:T(8,128)(2,1)S(1)} %copy-done), custom_call_target="tpu_custom_call" | custom-call | flops 5368709120 | bytes 20971520 | tf_op jit(solution)/shard_map/score/pallas_call | solution.py:246
  33.8 3.6 %all-to-all-start.1 = ((f32[128,1,128]{2,1,0:T(1,128)}), f32[128,1,128]{2,1,0:T(1,128)S(1)}, u32[]{:S(2)}, u32[]{:S(2)}) async-start(f32[128,1,128]{2,1,0:T(1,128)} %bitcast.5), calls=%async_computation.1 | async-start | bytes 131072 | tf_op jit(solution)/shard_map/all_to_all | solution.py:281
  37.4 2.1 %lookup.1.refs_1_ = s32[8,128]{1,0:T(8,128)S(1)} custom-call(s32[100,256]{1,0:T(8,128)} %bitcast.14, s32[2048,128]{1,0:T(8,128)} %bitcast.12, s32[16,256]{1,0:T(8,128)} %bitcast.15, s32[2,128]{1,0:T(2,128)} %bitcast.16), custom_call_target="tpu_custom_call" | custom-call | bytes 2097152 | tf_op jit(solution)/shard_map/lookup/pallas_call | solution.py:263
  39.5 7.5 %all-to-all-done.1 = f32[128,1,128]{2,1,0:T(1,128)S(1)} async-done(((f32[128,1,128]{2,1,0:T(1,128)}), f32[128,1,128]{2,1,0:T(1,128)S(1)}, u32[]{:S(2)}, u32[]{:S(2)}) %all-to-all-start.1) | async-done | bytes 65568 | tf_op jit(solution)/shard_map/all_to_all | solution.py:281
  47.0 0.8 %place.1 = (f32[2,16]{1,0:T(2,128)}, f32[2,100]{1,0:T(2,128)}) custom-call(f32[128,128]{1,0:T(8,128)S(1)} %bitcast.10, s32[8,128]{1,0:T(8,128)S(1)} %lookup.1.refs_1_), custom_call_target="tpu_custom_call" | custom-call | tf_op jit(solution)/shard_map/place/pallas_call | solution.py:282
  (1 shorter events, 0.0 us)
Async XLA Ops:
  0.6 26.2 %slice-start = ((s8[16777216]{0:T(1024)(128)(4,1)}), s8[4194304]{0:T(1024)(128)(4,1)S(1)}, s32[]{:S(2)}) async-start(s8[16777216]{0:T(1024)(128)(4,1)} %bitcast.8), calls=%async_computation.2 | async-start | bytes 8388608
  0.6 26.2 %slice-start.1 = ((s8[16777216]{0:T(1024)(128)(4,1)}), s8[4194304]{0:T(1024)(128)(4,1)S(1)}, s32[]{:S(2)}) async-start(s8[16777216]{0:T(1024)(128)(4,1)} %bitcast.8), calls=%async_computation.3 | async-start | bytes 8388608
  0.7 26.2 %slice-start.2 = ((s8[16777216]{0:T(1024)(128)(4,1)}), s8[4194304]{0:T(1024)(128)(4,1)S(1)}, s32[]{:S(2)}) async-start(s8[16777216]{0:T(1024)(128)(4,1)} %bitcast.8), calls=%async_computation.4 | async-start | bytes 8388608
  0.7 26.2 %slice-start.3 = ((s8[16777216]{0:T(1024)(128)(4,1)}), s8[4194304]{0:T(1024)(128)(4,1)S(1)}, s32[]{:S(2)}) async-start(s8[16777216]{0:T(1024)(128)(4,1)} %bitcast.8), calls=%async_computation.5 | async-start | bytes 8388608
  0.7 26.2 %copy-start = (bf16[2048,1024]{1,0:T(8,128)(2,1)S(1)}, bf16[2048,1024]{1,0:T(8,128)(2,1)}, u32[]{:S(2)}) copy-start(bf16[2048,1024]{1,0:T(8,128)(2,1)} %refs_4_.1) | copy-start | bytes 12582916
  26.2 2.3 %collective-permute-start = (bf16[128,2,640]{2,1,0:T(2,128)(2,1)S(1)}, bf16[128,2,640]{2,1,0:T(2,128)(2,1)S(1)}, u32[]{:S(2)}, u32[]{:S(2)}) collective-permute-start(bf16[128,2,640]{2,1,0:T(2,128)(2,1)S(1)} %all_to_all.10.got_ref.refs_0_), channel_id=1, source_target_pairs={{0,16},{16,0},{32,48},{48,32},{64,80},{80,64},{96,112},{112,96},{1... | collective-permute-start | bytes 983048 | tf_op jit(solution)/shard_map/ppermute | solution.py:233
  33.8 13.2 %all-to-all-start.1 = ((f32[128,1,128]{2,1,0:T(1,128)}), f32[128,1,128]{2,1,0:T(1,128)S(1)}, u32[]{:S(2)}, u32[]{:S(2)}) async-start(f32[128,1,128]{2,1,0:T(1,128)} %bitcast.5), calls=%async_computation.1 | async-start | bytes 131072 | tf_op jit(solution)/shard_map/all_to_all | solution.py:281

commit v5 on v4

--- a/solution.py
+++ b/solution.py
@@ -139,7 +139,7 @@
     core = lax.axis_index("row") & 1
     queries = jnp.concatenate([jnp.where(core == 0, mine, theirs), jnp.where(core == 0, theirs, mine)], axis=1)
     rest = pl.ds(pl.multiple_of((1 - core) * half, half), half)
-    digits = jnp.transpose(got[:, half:].astype(jnp.float32))
+    digits = jnp.transpose(got[:, half:].astype(jnp.float32)[:, :8])
     odd = lax.broadcasted_iota(jnp.int32, (1, count), 1) & 1 == 1
     digits = jnp.where(odd, digits[4:8, :], digits[0:4, :])
     one = (digits[0:1, :] * 256.0 + digits[1:2, :]).astype(jnp.int32)
@@ -172,8 +172,8 @@
     results.append(jnp.sum(second, axis=0, keepdims=True))
     results = jnp.concatenate(results, axis=0)
     results = jnp.concatenate([results, pltpu.roll(results, count - 1, 1)], axis=0)
-    results = jnp.concatenate([results, jnp.zeros((LANES - results.shape[0], count), jnp.float32)], axis=0)
-    wide_ref[...] = jnp.transpose(results)
+    wide_ref[:, : results.shape[0]] = jnp.transpose(results)
+    wide_ref[:, results.shape[0] :] = jnp.zeros((count, LANES - results.shape[0]), jnp.float32)
     out_ref[...] = wide_ref[pl.ds(0, out_ref.shape[0], stride=2), :]
 
 

time: 48 us -> 48 us (level)
  no operation moved by 1% of the time
where the time goes in v5:
time: 48 us; the launch traced here: 47.8 us
  blocking collectives  23.2 us (48%)
  Pallas kernels  12 us (25%)
  waiting for transfers between devices  7.5 us (16%)
  starting transfers between devices  4.32 us (9%)
  between operations  0.73 us (2%)
    all_to_all x1, blocking collectives, local(): got = lax.all_to_all(send, AXES, 0, 0, tiled=True)  23.2 us
    all_to_all x1, waiting for transfers between devices, local(): back = lax.all_to_all(results[:, None, :], AXES, 0, 0, tiled=True)[:, 0, :]  7.5 us
    pallas_call x1, Pallas kernels, local(): pl.pallas_call(lambda *refs: score_kernel(scale, *refs), out_shape=pltpu....  5.31 us
    all_to_all x1, starting transfers between devices, local(): back = lax.all_to_all(results[:, None, :], AXES, 0, 0, tiled=True)[:, 0, :]  3.62 us
    pallas_call x1, Pallas kernels, local(): pl.pallas_call(lambda *refs: pack_kernel(held_items, AXES, run, *refs), o...  2.24 us
    pallas_call x1, Pallas kernels, local(): pl.pallas_call(lambda *refs: lookup_kernel(held_items, AXES, mine, *refs)...  2.09 us
    pallas_call x1, Pallas kernels, local(): pl.pallas_call(early_kernel, out_shape=pltpu.VMEM((held_items + EARLY, de...  1.56 us
  transfers between devices with their start and end apart: 2, of which 1 were waited for; matrix products, arithmetic and copies ran while one was open for 0% of the time, Pallas kernels for 8%

profile of v5, /device:TPU:1, one launch (start us, length us, event | category | flops | bytes accessed | tf_op | source)
XLA Modules:
  0.0 47.8 jit_solution(12185132311324089577)
XLA Ops:
  0.6 0.0 slice-start
  0.6 0.0 slice-start.1
  0.7 0.0 slice-start.2
  0.7 0.0 slice-start.3
  0.7 0.0 copy-start
  0.7 2.2 %pack.1 = bf16[128,2,640]{2,1,0:T(2,128)(2,1)S(1)} custom-call(bf16[2,1024]{1,0:T(2,128)(2,1)} %refs_0_.1, s32[100,256]{1,0:T(8,128)} %bitcast.13, s32[2048,128]{1,0:T(8,128)} %bitcast.11), custom_call_target="tpu_custom_call" | custom-call | flops 68719476736 | bytes 268435456 | tf_op jit(solution)/shard_map/pack/pallas_call | solution.py:214
  2.9 23.2 %all_to_all.10.got_ref.refs_0_ = bf16[128,2,640]{2,1,0:T(2,128)(2,1)S(1)} all-to-all(bf16[128,2,640]{2,1,0:T(2,128)(2,1)S(1)} %pack.1), channel_id=1, replica_groups=mesh['row'=8,'col'=16] {'row','col'}, dimensions={0} | all-to-all | bytes 655360 | tf_op jit(solution)/shard_map/all_to_all | solution.py:231
  26.2 0.7 %collective-permute-start = (bf16[128,2,640]{2,1,0:T(2,128)(2,1)S(1)}, bf16[128,2,640]{2,1,0:T(2,128)(2,1)S(1)}, u32[]{:S(2)}, u32[]{:S(2)}) collective-permute-start(bf16[128,2,640]{2,1,0:T(2,128)(2,1)S(1)} %all_to_all.10.got_ref.refs_0_), channel_id=1, source_target_pairs={{0,16},{16,0},{32,48},{48,32},{64,80},{80,64},{96,112},{112,96},{1... | collective-permute-start | bytes 983048 | tf_op jit(solution)/shard_map/ppermute | solution.py:233
  26.9 0.0 slice-done
  26.9 0.0 slice-done.1
  26.9 0.0 slice-done.2
  26.9 0.0 slice-done.3
  26.9 0.0 copy-done
  26.9 1.6 %early.1.refs_2_ = f32[5120,256]{1,0:T(8,128)S(1)} custom-call(bf16[128,2,640]{2,1,0:T(2,128)(2,1)S(1)} %all_to_all.10.got_ref.refs_0_, bf16[2,4096,1024]{2,1,0:T(8,128)(2,1)S(1)} %bitcast.9, bf16[2048,1024]{1,0:T(8,128)(2,1)S(1)} %copy-done), custom_call_target="tpu_custom_call" | custom-call | flops 1342177280 | bytes 5242880 | tf_op jit(solution)/shard_map/early/pallas_call | solution.py:234
  28.5 0.0 collective-permute-done.refs_1_
  28.5 5.3 %score.1 = f32[128,128]{1,0:T(8,128)} custom-call(bf16[128,2,640]{2,1,0:T(2,128)(2,1)S(1)} %all_to_all.10.got_ref.refs_0_, bf16[128,2,640]{2,1,0:T(2,128)(2,1)S(1)} %collective-permute-done.refs_1_, f32[5120,256]{1,0:T(8,128)S(1)} %early.1.refs_2_, bf16[2,4096,1024]{2,1,0:T(8,128)(2,1)S(1)} %bitcast.9, bf16[2048,1024]{1,0:T(8,128)(2,1)S(1)} %copy-done), custom_call_target="tpu_custom_call" | custom-call | flops 5368709120 | bytes 20971520 | tf_op jit(solution)/shard_map/score/pallas_call | solution.py:246
  33.8 3.6 %all-to-all-start.1 = ((f32[128,1,128]{2,1,0:T(1,128)}), f32[128,1,128]{2,1,0:T(1,128)S(1)}, u32[]{:S(2)}, u32[]{:S(2)}) async-start(f32[128,1,128]{2,1,0:T(1,128)} %bitcast.5), calls=%async_computation.1 | async-start | bytes 131072 | tf_op jit(solution)/shard_map/all_to_all | solution.py:281
  37.4 2.1 %lookup.1.refs_1_ = s32[8,128]{1,0:T(8,128)S(1)} custom-call(s32[100,256]{1,0:T(8,128)} %bitcast.14, s32[2048,128]{1,0:T(8,128)} %bitcast.12, s32[16,256]{1,0:T(8,128)} %bitcast.15, s32[2,128]{1,0:T(2,128)} %bitcast.16), custom_call_target="tpu_custom_call" | custom-call | bytes 2097152 | tf_op jit(solution)/shard_map/lookup/pallas_call | solution.py:263
  39.5 7.5 %all-to-all-done.1 = f32[128,1,128]{2,1,0:T(1,128)S(1)} async-done(((f32[128,1,128]{2,1,0:T(1,128)}), f32[128,1,128]{2,1,0:T(1,128)S(1)}, u32[]{:S(2)}, u32[]{:S(2)}) %all-to-all-start.1) | async-done | bytes 65568 | tf_op jit(solution)/shard_map/all_to_all | solution.py:281
  47.0 0.8 %place.1 = (f32[2,16]{1,0:T(2,128)}, f32[2,100]{1,0:T(2,128)}) custom-call(f32[128,128]{1,0:T(8,128)S(1)} %bitcast.10, s32[8,128]{1,0:T(8,128)S(1)} %lookup.1.refs_1_), custom_call_target="tpu_custom_call" | custom-call | tf_op jit(solution)/shard_map/place/pallas_call | solution.py:282
  (1 shorter events, 0.0 us)
Async XLA Ops:
  0.6 26.2 %slice-start = ((s8[16777216]{0:T(1024)(128)(4,1)}), s8[4194304]{0:T(1024)(128)(4,1)S(1)}, s32[]{:S(2)}) async-start(s8[16777216]{0:T(1024)(128)(4,1)} %bitcast.8), calls=%async_computation.2 | async-start | bytes 8388608
  0.6 26.2 %slice-start.1 = ((s8[16777216]{0:T(1024)(128)(4,1)}), s8[4194304]{0:T(1024)(128)(4,1)S(1)}, s32[]{:S(2)}) async-start(s8[16777216]{0:T(1024)(128)(4,1)} %bitcast.8), calls=%async_computation.3 | async-start | bytes 8388608
  0.7 26.2 %slice-start.2 = ((s8[16777216]{0:T(1024)(128)(4,1)}), s8[4194304]{0:T(1024)(128)(4,1)S(1)}, s32[]{:S(2)}) async-start(s8[16777216]{0:T(1024)(128)(4,1)} %bitcast.8), calls=%async_computation.4 | async-start | bytes 8388608
  0.7 26.2 %slice-start.3 = ((s8[16777216]{0:T(1024)(128)(4,1)}), s8[4194304]{0:T(1024)(128)(4,1)S(1)}, s32[]{:S(2)}) async-start(s8[16777216]{0:T(1024)(128)(4,1)} %bitcast.8), calls=%async_computation.5 | async-start | bytes 8388608
  0.7 26.2 %copy-start = (bf16[2048,1024]{1,0:T(8,128)(2,1)S(1)}, bf16[2048,1024]{1,0:T(8,128)(2,1)}, u32[]{:S(2)}) copy-start(bf16[2048,1024]{1,0:T(8,128)(2,1)} %refs_4_.1) | copy-start | bytes 12582916
  26.2 2.3 %collective-permute-start = (bf16[128,2,640]{2,1,0:T(2,128)(2,1)S(1)}, bf16[128,2,640]{2,1,0:T(2,128)(2,1)S(1)}, u32[]{:S(2)}, u32[]{:S(2)}) collective-permute-start(bf16[128,2,640]{2,1,0:T(2,128)(2,1)S(1)} %all_to_all.10.got_ref.refs_0_), channel_id=1, source_target_pairs={{0,16},{16,0},{32,48},{48,32},{64,80},{80,64},{96,112},{112,96},{1... | collective-permute-start | bytes 983048 | tf_op jit(solution)/shard_map/ppermute | solution.py:233
  33.8 13.2 %all-to-all-start.1 = ((f32[128,1,128]{2,1,0:T(1,128)}), f32[128,1,128]{2,1,0:T(1,128)S(1)}, u32[]{:S(2)}, u32[]{:S(2)}) async-start(f32[128,1,128]{2,1,0:T(1,128)} %bitcast.5), calls=%async_computation.1 | async-start | bytes 131072 | tf_op jit(solution)/shard_map/all_to_all | solution.py:281
